TPU v7x, 32 devices: a whole 2x2x4 slice. The times are simulated.
32 devices in a mesh: gx: 4 (over y, x), gy: 8 (over z, core).
Axes of the slice: x: 2, y: 2, z: 4, core: 2. Of those that a mesh axis runs over, the one named last changes fastest.
Arguments:
- starting_sag: float32 [512, 1024], P('gx', 'gy'), may hold values from -6 to 6
- warmth_celsius_field: float32 [512, 1024], P('gx', 'gy'), may hold values from 25 to 125
- junction_charge_store: float32 [512, 1024], P('gx', 'gy'), may hold values from 5e-05 to 0.0005
- load_amperes: float32 [2, 512, 1024], P(None, 'gx', 'gy'), may hold values from -0.08 to 0.08
- source_patch_bits: int32 [16, 32], P('gx', 'gy'), may hold values 0 or 1
Outputs:
- drop: float32 [512, 1024], P('gx', 'gy')
All inputs are finite; a program needn't handle non-finite values. No bound on the sum of `source_patch_bits` on one device may be relied on, other than what follows from the above.
Results may differ from a plain program's by a relative error of at most 0.0013.
Values sent between devices are 32-bit elements; how exact they have to be, the bound alone decides.
A program may use at most 64 MiB of HBM per device.

v0:
```python
import jax
import jax.numpy as jnp
from jax import lax
from jax.sharding import PartitionSpec as P

STEPS = 2
PITCH = 32


xward_admittance = 1.0
yward_admittance = 0.5
warmth_scaling = 0.004
surrounding_warmth = 25.0
cushion_pieces = 1.0


def with_halo(x, sides, width):
    for axis, dim in sides:
        devices, length = (lax.axis_size(axis), x.shape[dim])
        up = [(i, (i + 1) % devices) for i in range(devices - 1)]
        down = [(j, i) for i, j in up]
        last = lax.slice_in_dim(x, length - width, length, axis=dim)
        first = lax.slice_in_dim(x, 0, width, axis=dim)
        before = lax.ppermute(last, axis, up)
        after = lax.ppermute(first, axis, down)
        x = jnp.concatenate([before, x, after], axis=dim)
    return x


def factor(sub_diag, main_diag, sup_diag):

    def advance(prev_ratio, packed):
        sub_row, main_row, sup_row = packed
        pivot_row = 1.0 / (main_row - sub_row * prev_ratio)
        next_ratio = sup_row * pivot_row
        return (next_ratio, (pivot_row, next_ratio))

    _, (pivots, ratios) = lax.scan(
        advance, jnp.zeros_like(main_diag[0]), (sub_diag, main_diag, sup_diag)
    )
    return (pivots, ratios)


def substitute(sub_diag, pivots, ratios, source):

    def forward(prev_value, packed):
        sub_row, pivot_row, source_row = packed
        new_value = (source_row - sub_row * prev_value) * pivot_row
        return (new_value, new_value)

    _, partial_sol = lax.scan(forward, jnp.zeros_like(source[0]), (sub_diag, pivots, source))

    def backward(next_value, packed):
        ratio_row, partial_row = packed
        new_value = partial_row - ratio_row * next_value
        return (new_value, new_value)

    _, solved = lax.scan(backward, jnp.zeros_like(source[0]), (ratios, partial_sol), reverse=True)
    return solved


def spike_pair(lower, upper, pivots, ratios):
    length = lower.shape[0]
    row_ids = jnp.arange(length)[:, None]
    spike_upper = jnp.where(row_ids == length - 1, upper[-1][None, :], 0.0)
    spike_lower = jnp.where(row_ids == 0, lower[0][None, :], 0.0)
    spikes = substitute(-lower, pivots, ratios, jnp.stack([spike_upper, spike_lower], 1))
    return (spikes[:, 0], spikes[:, 1])


def relation(local_sol, reach_next, reach_prev):
    return jnp.stack(
        [local_sol[0], local_sol[-1], reach_next[0], reach_next[-1], reach_prev[0], reach_prev[-1]]
    )


def join(left_part, right_part):
    scaled = 1.0 / (1.0 - left_part[3] * right_part[4])
    last_base = (left_part[1] + left_part[3] * right_part[0]) * scaled
    last_right = left_part[3] * right_part[2] * scaled
    last_left = left_part[5] * scaled
    first_base = right_part[0] + right_part[4] * last_base
    first_right = right_part[2] + right_part[4] * last_right
    first_left = right_part[4] * last_left
    return jnp.stack(
        [
            left_part[0] + left_part[2] * first_base,
            right_part[1] + right_part[5] * last_base,
            left_part[2] * first_right,
            right_part[3] + right_part[5] * last_right,
            left_part[4] + left_part[2] * first_left,
            right_part[5] * last_left,
        ]
    )


def junction(left_part, right_part):
    scaled = 1.0 / (1.0 - left_part[3] * right_part[4])
    last_base = (left_part[1] + left_part[3] * right_part[0]) * scaled
    return (last_base, right_part[0] + right_part[4] * last_base)


def every_side(gathered, identity):

    def extend_left(running, member):
        return (join(running, member), running)

    _, prefix = lax.scan(extend_left, identity, gathered)

    def extend_right(running, member):
        return (join(member, running), running)

    _, suffix = lax.scan(extend_right, identity, gathered, reverse=True)
    return (prefix, suffix)


def finish(local_sol, own_rel, from_left, from_right, reach_next, reach_prev):
    left_last, _ = junction(from_left, join(own_rel, from_right))
    _, right_first = junction(join(from_left, own_rel), from_right)
    return local_sol + reach_next * right_first + reach_prev * left_last


def unit_relation(width):
    return jnp.broadcast_to(
        jnp.array([0.0, 0.0, 1.0, 0.0, 0.0, 1.0], jnp.float32)[:, None], (6, width)
    )


def local(
    starting_sag, warmth_celsius_field, junction_charge_store, load_amperes, source_patch_bits
):
    rows_dev, cols_dev = starting_sag.shape
    count_x = lax.axis_size("gx")
    count_y = lax.axis_size("gy")
    place_x = lax.axis_index("gx")
    place_y = lax.axis_index("gy")
    width_col = rows_dev // count_y
    rim_allowance = with_halo(warmth_celsius_field, (("gx", 0), ("gy", 1)), 1)
    inner_x = rim_allowance[:, 1:-1]
    xward_wire = xward_admittance / (
        1.0 + warmth_scaling * (0.5 * (inner_x[:-1] + inner_x[1:]) - surrounding_warmth)
    )
    row_pos = jnp.arange(rows_dev + 1)[:, None]
    outside_x = (place_x == 0) & (row_pos == 0) | (place_x == count_x - 1) & (row_pos == rows_dev)
    xward_wire = jnp.where(outside_x, 0.0, xward_wire)
    inner_y = rim_allowance[1:-1]
    yward_wire = yward_admittance / (
        1.0 + warmth_scaling * (0.5 * (inner_y[:, :-1] + inner_y[:, 1:]) - surrounding_warmth)
    )
    col_pos = jnp.arange(cols_dev + 1)[None, :]
    outside_y = (place_y == 0) & (col_pos == 0) | (place_y == count_y - 1) & (col_pos == cols_dev)
    yward_wire = jnp.where(outside_y, 0.0, yward_wire)
    left_x = xward_wire[:-1]
    right_x = xward_wire[1:]
    left_y = yward_wire[:, :-1]
    right_y = yward_wire[:, 1:]
    flag_vals = source_patch_bits.astype(jnp.float32)
    first_pos = (jnp.arange(PITCH) == 0).astype(jnp.float32)
    semi_cushion = cushion_pieces * (
        flag_vals[:, None, :, None]
        * first_pos[None, :, None, None]
        * first_pos[None, None, None, :]
    ).reshape(rows_dev, cols_dev)
    diag_x = junction_charge_store + left_x + right_x + semi_cushion
    pivots_x, ratios_x = factor(-left_x, diag_x, -right_x)
    reach_right, reach_left = spike_pair(left_x, right_x, pivots_x, ratios_x)
    cap_col, pad_col, lower_col, upper_col = (
        lax.all_to_all(junction_charge_store.T, "gy", split_axis=1, concat_axis=1, tiled=True),
        lax.all_to_all(semi_cushion.T, "gy", split_axis=1, concat_axis=1, tiled=True),
        lax.all_to_all(left_y.T, "gy", split_axis=1, concat_axis=1, tiled=True),
        lax.all_to_all(right_y.T, "gy", split_axis=1, concat_axis=1, tiled=True),
    )
    diag_col = cap_col + lower_col + upper_col + pad_col
    pivots_y, ratios_y = factor(-lower_col, diag_col, -upper_col)
    reach_up, reach_down = spike_pair(lower_col, upper_col, pivots_y, ratios_y)
    identity = unit_relation(cols_dev)
    block_identity = unit_relation(width_col)
    drop_now = starting_sag
    carried = starting_sag
    for step_index in range(STEPS):
        if step_index > 0:
            source = carried + load_amperes[step_index]
        else:
            padded = with_halo(drop_now, (("gy", 1),), 1)
            source = (
                junction_charge_store * drop_now
                - (
                    right_y * (drop_now - padded[:, 2:])
                    + left_y * (drop_now - padded[:, :-2])
                    + semi_cushion * drop_now
                )
                + load_amperes[step_index]
            )
        solve_local_sol = substitute(-left_x, pivots_x, ratios_x, source)
        solve_own_rel = relation(solve_local_sol, reach_right, reach_left)
        gathered = lax.all_gather(solve_own_rel[None], "gx", axis=0, tiled=True)
        solve_prefix, solve_suffix = every_side(gathered, identity)
        from_left = lax.dynamic_index_in_dim(solve_prefix, place_x, 0, False)
        from_right = lax.dynamic_index_in_dim(solve_suffix, place_x, 0, False)
        half_drop = finish(
            solve_local_sol, solve_own_rel, from_left, from_right, reach_right, reach_left
        )
        operate_padded = with_halo(half_drop, (("gx", 0),), 1)
        source = (
            junction_charge_store * half_drop
            - (
                right_x * (half_drop - operate_padded[2:])
                + left_x * (half_drop - operate_padded[:-2])
                + semi_cushion * half_drop
            )
            + load_amperes[step_index]
        )
        column_src = lax.all_to_all(source.T, "gy", split_axis=1, concat_axis=1, tiled=True)
        local_sol = substitute(-lower_col, pivots_y, ratios_y, column_src)
        own_rel = relation(local_sol, reach_up, reach_down)
        blocks = own_rel.reshape(6, count_y, width_col).transpose(1, 0, 2)
        prefix, suffix = every_side(blocks, block_identity)
        from_low = prefix.transpose(1, 0, 2).reshape(6, rows_dev)
        from_high = suffix.transpose(1, 0, 2).reshape(6, rows_dev)
        column_drop = finish(local_sol, own_rel, from_low, from_high, reach_up, reach_down)
        keep_going = step_index + 1 < STEPS
        if keep_going:
            blank = jnp.zeros((width_col,), column_drop.dtype)
            after = jnp.concatenate([column_drop[0, width_col:], blank])[None]
            before = jnp.concatenate([blank, column_drop[-1, :-width_col]])[None]
            next_rows = jnp.concatenate([column_drop[1:], after], 0)
            prev_rows = jnp.concatenate([before, column_drop[:-1]], 0)
            payload = cap_col * column_drop - (
                upper_col * (column_drop - next_rows)
                + lower_col * (column_drop - prev_rows)
                + pad_col * column_drop
            )
        else:
            payload = column_drop
        line_drop = lax.all_to_all(payload, "gy", split_axis=1, concat_axis=1, tiled=True).T
        if keep_going:
            carried = line_drop
        else:
            drop_now = line_drop
    return drop_now


def solution(mesh):
    return jax.shard_map(
        local,
        mesh=mesh,
        in_specs=(P("gx", "gy"), P("gx", "gy"), P("gx", "gy"), P(None, "gx", "gy"), P("gx", "gy")),
        out_specs=P("gx", "gy"),
        check_vma=False,
    )
```

profile of v0, /device:TPU:0, one launch (start us, length us, event | category | flops | bytes accessed | tf_op | source)
XLA Modules:
  0.0 268.4 jit_solution(5435071564994925096)
XLA Ops:
  0.0 0.7 fusion.293
  0.7 4.8 %collective-permute-start = (f32[1,128]{1,0:T(1,128)S(1)}, f32[1,128]{1,0:T(1,128)S(1)}, u32[]{:S(2)}, u32[]{:S(2)}) collective-permute-start(f32[1,128]{1,0:T(1,128)S(1)} %get-tuple-element.2141), channel_id=1, source_target_pairs={{0,8},{8,16},{16,24},{1,9},{9,17},{17,25},{2,10},{10,18},{18,26},{... | collective-permute-start | bytes 1544 | tf_op jit(solution)/shard_map/ppermute | solution.py:24
  5.6 1.3 collective-permute-start.1
  6.9 1.0 fusion.294
  7.9 1.3 collective-permute-start.4
  9.1 3.0 %collective-permute-start.5 = (f32[128,1]{1,0:T(8,128)S(1)}, f32[128,1]{1,0:T(8,128)S(1)}, u32[]{:S(2)}, u32[]{:S(2)}) collective-permute-start(f32[128,1]{1,0:T(8,128)S(1)} %get-tuple-element.2143), channel_id=1, source_target_pairs={{0,1},{1,2},{2,3},{3,4},{4,5},{5,6},{6,7},{8,9},{9,10},{10,11},{11... | collective-permute-start | bytes 1544 | tf_op jit(solution)/shard_map/ppermute | solution.py:24
  12.3 0.7 copy-done.4
  13.1 0.2 mul.2036
  13.3 0.2 mul.2037
  13.6 0.6 copy-done
  14.2 3.1 %collective-permute-start.2 = (f32[130,1]{1,0:T(8,128)S(1)}, f32[130,1]{1,0:T(8,128)S(1)}, u32[]{:S(2)}, u32[]{:S(2)}) collective-permute-start(f32[130,1]{1,0:T(8,128)S(1)} %get-tuple-element.2125), channel_id=1, source_target_pairs={{0,1},{1,2},{2,3},{3,4},{4,5},{5,6},{6,7},{8,9},{9,10},{10,11},{11... | collective-permute-start | bytes 1568 | tf_op jit(solution)/shard_map/ppermute | solution.py:24
  17.3 1.3 collective-permute-start.3
  18.7 1.5 add_add_fusion
  20.2 14.5 %while.330 = (s32[]{:T(128)}, f32[128]{0:T(128)S(1)}, f32[128,128]{1,0:T(8,128)S(1)}, f32[128,128]{1,0:T(8,128)S(1)}, f32[128,128]{1,0:T(8,128)S(1)}, /*index=5*...) while((s32[]{:T(128)}, f32[128]{0:T(128)S(1)}, f32[128,128]{1,0:T(8,128)S(1)}, ...), condition=%wide.region_3.4_spmd.clone, body=%wide.region_2.3_spmd.clone.sunk | while | flops 643 | bytes 5235 | solution.py:38
  34.9 0.6 copy-done.1
  35.7 1.6 fusion.286
  37.3 6.0 %all-to-all-start.3 = ((f32[128,8,16]{0,2,1:T(8,128)}), f32[128,8,16]{0,2,1:T(8,128)S(1)}, u32[]{:S(2)}, u32[]{:S(2)}) async-start(f32[128,8,16]{0,2,1:T(8,128)} %bitcast.82), calls=%async_computation.3 | async-start | bytes 131072 | tf_op jit(solution)/shard_map/all_to_all | solution.py:171
  43.4 9.6 %while.331 = (s32[]{:T(128)}, f32[128]{0:T(128)S(1)}, f32[128,128]{1,0:T(8,128)S(1)}, f32[128,128]{1,0:T(8,128)S(1)}, f32[128,128]{1,0:T(8,128)S(1)}, /*index=5*/f32[128,128]{1,0:T(8,128)S(1)}, s32[]{:T(128)}, s32[]{:T(128)}) while((s32[]{:T(128)}, f32[128]{0:T(128)S(1)}, f32[128,128]{1,0:T(8,128)S(1)}, f32[128,128]{1,0:T(8,128)S(1)}, ...), condition=%wide.region_5.6_spmd.clone, body=%wide.region_4.5_spmd.clone.sunk | while | flops 515 | bytes 3687 | solution.py:51
  53.0 9.6 %while.332 = (s32[]{:T(128)}, f32[128]{0:T(128)S(1)}, f32[128,128]{1,0:T(8,128)S(1)}, f32[128,128]{1,0:T(8,128)S(1)}, f32[128,128]{1,0:T(8,128)S(1)}, /*index=5*/s32[]{:T(128)}, s32[]{:T(128)}, s32[]{:T(128)}) while((s32[]{:T(128)}, f32[128]{0:T(128)S(1)}, f32[128,128]{1,0:T(8,128)S(1)}, f32[128,128]{1,0:T(8,128)S(1)}, ...), condition=%wide.region_7.8_spmd.clone, body=%wide.region_6.7_spmd.clone.sunk | while | flops 388 | bytes 3187 | solution.py:58
  62.7 5.1 %all-to-all-start.2 = ((f32[128,8,16]{0,2,1:T(8,128)}), f32[128,8,16]{0,2,1:T(8,128)S(1)}, u32[]{:S(2)}, u32[]{:S(2)}) async-start(f32[128,8,16]{0,2,1:T(8,128)} %bitcast.79), calls=%async_computation.2 | async-start | bytes 131072 | tf_op jit(solution)/shard_map/all_to_all | solution.py:170
  67.8 0.2 slice_reduce_fusion.1
  68.1 5.7 %all-to-all-done.2 = f32[128,8,16]{0,2,1:T(8,128)S(1)} async-done(((f32[128,8,16]{0,2,1:T(8,128)}), f32[128,8,16]{0,2,1:T(8,128)S(1)}, u32[]{:S(2)}, u32[]{:S(2)}) %all-to-all-start.2) | async-done | bytes 65568 | tf_op jit(solution)/shard_map/all_to_all | solution.py:170
  73.7 3.4 %all-to-all-start = ((f32[128,8,16]{0,2,1:T(8,128)}), f32[128,8,16]{0,2,1:T(8,128)S(1)}, u32[]{:S(2)}, u32[]{:S(2)}) async-start(f32[128,8,16]{0,2,1:T(8,128)} %bitcast.57), calls=%async_computation | async-start | bytes 131072 | tf_op jit(solution)/shard_map/all_to_all | solution.py:168
  77.3 0.3 broadcast_select_fusion.10
  77.8 7.3 %while.333 = (s32[]{:T(128)}, f32[2,128]{1,0:T(2,128)S(1)}, f32[128,2,128]{2,1,0:T(2,128)S(1)}, f32[128,2,128]{2,1,0:T(2,128)S(1)}, f32[128,128]{1,0:T(8,128)S(1...) while((s32[]{:T(128)}, f32[2,128]{1,0:T(2,128)S(1)}, f32[128,2,128]{2,1,0:T(2,128)S(1)}, ...), condition=%wide.region_9.10_spmd.clone, body=%wide.region_8.9_spmd.clone.sunk | while | flops 1027 | bytes 7271 | solution.py:51
  85.2 7.1 %while.334 = (s32[]{:T(128)}, f32[2,128]{1,0:T(2,128)S(1)}, f32[128,2,128]{2,1,0:T(2,128)S(1)}, f32[128,2,128]{2,1,0:T(2,128)S(1)}, f32[128,128]{1,0:T(8,128)S(1)}, /*index=5*/s32[]{:T(128)}, s32[]{:T(128)}, s32[]{:T(128)}) while((s32[]{:T(128)}, f32[2,128]{1,0:T(2,128)S(1)}, f32[128,2,128]{2,1,0:T(2,128)S(1)}, ...), condition=%wide.region_11.12_spmd.clone, body=%wide.region_10.11_spmd.clone.sunk | while | flops 772 | bytes 5747 | solution.py:58
  92.4 10.2 %all-gather.2 = f32[4,6,128]{2,1,0:T(8,128)S(1)} all-gather(f32[1,6,128]{2,1,0:T(8,128)S(1)} %bitcast.1238), channel_id=2, replica_groups=mesh['gx'=4,'gy'=8] {'gx'}, dimensions={0}, use_global_device_ids=true | all-gather | bytes 15360 | tf_op jit(solution)/shard_map/all_gather | solution.py:196
  102.6 0.7 copy-done.3
  103.3 0.4 while.322
  103.8 0.4 while.323
  104.3 5.0 %all-to-all-start.4 = ((f32[128,8,16]{0,2,1:T(8,128)}), f32[128,8,16]{0,2,1:T(8,128)S(1)}, u32[]{:S(2)}, u32[]{:S(2)}) async-start(f32[128,8,16]{0,2,1:T(8,128)} %bitcast.85), calls=%async_computation.4 | async-start | bytes 131072 | tf_op jit(solution)/shard_map/all_to_all | solution.py:169
  109.3 5.9 %all-to-all-done.4 = f32[128,8,16]{0,2,1:T(8,128)S(1)} async-done(((f32[128,8,16]{0,2,1:T(8,128)}), f32[128,8,16]{0,2,1:T(8,128)S(1)}, u32[]{:S(2)}, u32[]{:S(2)}) %all-to-all-start.4) | async-done | bytes 65568 | tf_op jit(solution)/shard_map/all_to_all | solution.py:169
  115.6 14.5 %while.335 = (s32[]{:T(128)}, f32[128]{0:T(128)S(1)}, f32[128,128]{1,0:T(8,128)S(1)}, f32[128,128]{1,0:T(8,128)S(1)}, f32[128,128]{1,0:T(8,128)S(1)}, /*index=5*...) while((s32[]{:T(128)}, f32[128]{0:T(128)S(1)}, f32[128,128]{1,0:T(8,128)S(1)}, ...), condition=%wide.region_1.2_spmd.clone, body=%wide.region_0.1_spmd.clone.sunk | while | flops 643 | bytes 5235 | solution.py:38
  130.1 1.3 collective-permute-start.6
  131.4 4.5 %collective-permute-start.7 = (f32[1,128]{1,0:T(1,128)S(1)}, f32[1,128]{1,0:T(1,128)S(1)}, u32[]{:S(2)}, u32[]{:S(2)}) collective-permute-start(f32[1,128]{1,0:T(1,128)S(1)} %get-tuple-element.2137), channel_id=1, source_target_pairs={{0,8},{8,16},{16,24},{1,9},{9,17},{17,25},{2,10},{10,18},{18,26},{... | collective-permute-start | bytes 1544 | tf_op jit(solution)/shard_map/ppermute | solution.py:24
  136.1 7.3 %while.338 = (s32[]{:T(128)}, f32[2,128]{1,0:T(2,128)S(1)}, f32[128,2,128]{2,1,0:T(2,128)S(1)}, f32[128,2,128]{2,1,0:T(2,128)S(1)}, f32[128,128]{1,0:T(8,128)S(1...) while((s32[]{:T(128)}, f32[2,128]{1,0:T(2,128)S(1)}, f32[128,2,128]{2,1,0:T(2,128)S(1)}, ...), condition=%wide.region_21.22_spmd.clone, body=%wide.region_20.21_spmd.clone.sunk | while | flops 1027 | bytes 7271 | solution.py:51
  143.5 1.5 fusion.156
  145.0 3.3 %all-to-all-start.1 = ((f32[128,8,16]{0,2,1:T(8,128)}), f32[128,8,16]{0,2,1:T(8,128)S(1)}, u32[]{:S(2)}, u32[]{:S(2)}) async-start(f32[128,8,16]{0,2,1:T(8,128)} %bitcast.76), calls=%async_computation.1 | async-start | bytes 131072 | tf_op jit(solution)/shard_map/all_to_all | solution.py:213
  148.4 7.1 %while.339 = (s32[]{:T(128)}, f32[2,128]{1,0:T(2,128)S(1)}, f32[128,2,128]{2,1,0:T(2,128)S(1)}, f32[128,2,128]{2,1,0:T(2,128)S(1)}, f32[128,128]{1,0:T(8,128)S(1)}, /*index=5*/s32[]{:T(128)}, s32[]{:T(128)}, s32[]{:T(128)}) while((s32[]{:T(128)}, f32[2,128]{1,0:T(2,128)S(1)}, f32[128,2,128]{2,1,0:T(2,128)S(1)}, ...), condition=%wide.region_23.24_spmd.clone, body=%wide.region_22.23_spmd.clone.sunk | while | flops 772 | bytes 5747 | solution.py:58
  156.2 9.6 %while.336 = (s32[]{:T(128)}, f32[128]{0:T(128)S(1)}, f32[128,128]{1,0:T(8,128)S(1)}, f32[128,128]{1,0:T(8,128)S(1)}, f32[128,128]{1,0:T(8,128)S(1)}, /*index=5*/f32[128,128]{1,0:T(8,128)S(1)}, s32[]{:T(128)}, s32[]{:T(128)}) while((s32[]{:T(128)}, f32[128]{0:T(128)S(1)}, f32[128,128]{1,0:T(8,128)S(1)}, ...), condition=%wide.region_17.18_spmd.clone, body=%wide.region_16.17_spmd.clone.sunk | while | flops 515 | bytes 3687 | solution.py:51
  165.8 9.6 %while.337 = (s32[]{:T(128)}, f32[128]{0:T(128)S(1)}, f32[128,128]{1,0:T(8,128)S(1)}, f32[128,128]{1,0:T(8,128)S(1)}, f32[128,128]{1,0:T(8,128)S(1)}, /*index=5*/s32[]{:T(128)}, s32[]{:T(128)}, s32[]{:T(128)}) while((s32[]{:T(128)}, f32[128]{0:T(128)S(1)}, f32[128,128]{1,0:T(8,128)S(1)}, f32[128,128]{1,0:T(8,128)S(1)}, ...), condition=%wide.region_19.20_spmd.clone, body=%wide.region_18.19_spmd.clone.sunk | while | flops 388 | bytes 3187 | solution.py:58
  175.9 0.9 while.325
  177.1 1.0 while.324
  178.5 0.2 slice_reduce_fusion.2
  179.0 0.7 fusion.170
  179.7 5.0 %all-to-all-start.5 = ((f32[128,8,16]{0,2,1:T(8,128)}), f32[128,8,16]{0,2,1:T(8,128)S(1)}, u32[]{:S(2)}, u32[]{:S(2)}) async-start(f32[128,8,16]{0,2,1:T(8,128)} %bitcast.100), calls=%async_computation.5 | async-start | bytes 131072 | tf_op jit(solution)/shard_map/all_to_all | solution.py:235
  184.7 5.9 %all-to-all-done.5 = f32[128,8,16]{0,2,1:T(8,128)S(1)} async-done(((f32[128,8,16]{0,2,1:T(8,128)}), f32[128,8,16]{0,2,1:T(8,128)S(1)}, u32[]{:S(2)}, u32[]{:S(2)}) %all-to-all-start.5) | async-done | bytes 65568 | tf_op jit(solution)/shard_map/all_to_all | solution.py:235
  190.7 9.6 %while.340 = (s32[]{:T(128)}, f32[128]{0:T(128)S(1)}, f32[128,128]{1,0:T(8,128)S(1)}, f32[128,128]{1,0:T(8,128)S(1)}, f32[128,128]{1,0:T(8,128)S(1)}, /*index=5*/f32[128,128]{1,0:T(8,128)S(1)}, s32[]{:T(128)}, s32[]{:T(128)}) while((s32[]{:T(128)}, f32[128]{0:T(128)S(1)}, f32[128,128]{1,0:T(8,128)S(1)}, ...), condition=%wide.region_29.30_spmd.clone, body=%wide.region_28.29_spmd.clone.sunk | while | flops 515 | bytes 3687 | solution.py:51
  200.3 9.6 %while.341 = (s32[]{:T(128)}, f32[128]{0:T(128)S(1)}, f32[128,128]{1,0:T(8,128)S(1)}, f32[128,128]{1,0:T(8,128)S(1)}, f32[128,128]{1,0:T(8,128)S(1)}, /*index=5*/s32[]{:T(128)}, s32[]{:T(128)}, s32[]{:T(128)}) while((s32[]{:T(128)}, f32[128]{0:T(128)S(1)}, f32[128,128]{1,0:T(8,128)S(1)}, f32[128,128]{1,0:T(8,128)S(1)}, ...), condition=%wide.region_31.32_spmd.clone, body=%wide.region_30.31_spmd.clone.sunk | while | flops 388 | bytes 3187 | solution.py:58
  210.0 8.1 %all-gather.3 = f32[4,6,128]{2,1,0:T(8,128)S(1)} all-gather(f32[1,6,128]{2,1,0:T(8,128)S(1)} %bitcast.1237), channel_id=3, replica_groups=mesh['gx'=4,'gy'=8] {'gx'}, dimensions={0}, use_global_device_ids=true | all-gather | bytes 15360 | tf_op jit(solution)/shard_map/all_gather | solution.py:196
  218.2 0.4 while.326
  218.7 0.4 while.327
  219.2 1.3 collective-permute-start.8
  220.5 4.5 %collective-permute-start.9 = (f32[1,128]{1,0:T(1,128)S(1)}, f32[1,128]{1,0:T(1,128)S(1)}, u32[]{:S(2)}, u32[]{:S(2)}) collective-permute-start(f32[1,128]{1,0:T(1,128)S(1)} %get-tuple-element.2128), channel_id=1, source_target_pairs={{0,8},{8,16},{16,24},{1,9},{9,17},{17,25},{2,10},{10,18},{18,26},{... | collective-permute-start | bytes 1544 | tf_op jit(solution)/shard_map/ppermute | solution.py:24
  225.1 1.3 collective-permute-done.9
  226.4 1.5 fusion.148
  227.9 3.4 %all-to-all-start.6 = ((f32[128,8,16]{0,2,1:T(8,128)}), f32[128,8,16]{0,2,1:T(8,128)S(1)}, u32[]{:S(2)}, u32[]{:S(2)}) async-start(f32[128,8,16]{0,2,1:T(8,128)} %bitcast.112), calls=%async_computation.6 | async-start | bytes 131072 | tf_op jit(solution)/shard_map/all_to_all | solution.py:213
  231.3 5.8 %all-to-all-done.6 = f32[128,8,16]{0,2,1:T(8,128)S(1)} async-done(((f32[128,8,16]{0,2,1:T(8,128)}), f32[128,8,16]{0,2,1:T(8,128)S(1)}, u32[]{:S(2)}, u32[]{:S(2)}) %all-to-all-start.6) | async-done | bytes 65568 | tf_op jit(solution)/shard_map/all_to_all | solution.py:213
  237.2 9.6 %while.342 = (s32[]{:T(128)}, f32[128]{0:T(128)S(1)}, f32[128,128]{1,0:T(8,128)S(1)}, f32[128,128]{1,0:T(8,128)S(1)}, f32[128,128]{1,0:T(8,128)S(1)}, /*index=5*/f32[128,128]{1,0:T(8,128)S(1)}, s32[]{:T(128)}, s32[]{:T(128)}) while((s32[]{:T(128)}, f32[128]{0:T(128)S(1)}, f32[128,128]{1,0:T(8,128)S(1)}, ...), condition=%wide.region_37.38_spmd.clone, body=%wide.region_36.37_spmd.clone.sunk | while | flops 515 | bytes 3687 | solution.py:51
  246.9 9.6 %while.343 = (s32[]{:T(128)}, f32[128]{0:T(128)S(1)}, f32[128,128]{1,0:T(8,128)S(1)}, f32[128,128]{1,0:T(8,128)S(1)}, f32[128,128]{1,0:T(8,128)S(1)}, /*index=5*/s32[]{:T(128)}, s32[]{:T(128)}, s32[]{:T(128)}) while((s32[]{:T(128)}, f32[128]{0:T(128)S(1)}, f32[128,128]{1,0:T(8,128)S(1)}, f32[128,128]{1,0:T(8,128)S(1)}, ...), condition=%wide.region_39.40_spmd.clone, body=%wide.region_38.39_spmd.clone.sunk | while | flops 388 | bytes 3187 | solution.py:58
  256.9 0.9 while.329
  258.1 1.0 while.328
  259.5 8.3 %all_to_all.96 = f32[128,8,16]{0,2,1:T(8,128)S(1)} all-to-all(f32[128,8,16]{0,2,1:T(8,128)S(1)} %bitcast.1218), channel_id=1, replica_groups=mesh['gx'=4,'gy'=8] {'gy'}, dimensions={1} | all-to-all | bytes 131072 | tf_op jit(solution)/shard_map/all_to_all | solution.py:235
  267.8 0.6 copy.351
  (4235 shorter events, 105.6 us)
Async XLA Ops:
  0.7 12.9 %collective-permute-start = (f32[1,128]{1,0:T(1,128)S(1)}, f32[1,128]{1,0:T(1,128)S(1)}, u32[]{:S(2)}, u32[]{:S(2)}) collective-permute-start(f32[1,128]{1,0:T(1,128)S(1)} %get-tuple-element.2141), channel_id=1, source_target_pairs={{0,8},{8,16},{16,24},{1,9},{9,17},{17,25},{2,10},{10,18},{18,26},{... | collective-permute-start | bytes 1544 | tf_op jit(solution)/shard_map/ppermute | solution.py:24
  5.6 8.0 %collective-permute-start.1 = (f32[1,128]{1,0:T(1,128)S(1)}, f32[1,128]{1,0:T(1,128)S(1)}, u32[]{:S(2)}, u32[]{:S(2)}) collective-permute-start(f32[1,128]{1,0:T(1,128)S(1)} %get-tuple-element.2140), channel_id=1, source_target_pairs={{8,0},{16,8},{24,16},{9,1},{17,9},{25,17},{10,2},{18,10},{26,18},{... | collective-permute-start | bytes 1544 | tf_op jit(solution)/shard_map/ppermute | solution.py:25
  7.9 27.1 %collective-permute-start.4 = (f32[128,1]{1,0:T(8,128)S(1)}, f32[128,1]{1,0:T(8,128)S(1)}, u32[]{:S(2)}, u32[]{:S(2)}) collective-permute-start(f32[128,1]{1,0:T(8,128)S(1)} %get-tuple-element.2142), channel_id=1, source_target_pairs={{1,0},{2,1},{3,2},{4,3},{5,4},{6,5},{7,6},{9,8},{10,9},{11,10},{12... | collective-permute-start | bytes 1544 | tf_op jit(solution)/shard_map/ppermute | solution.py:25
  9.1 25.8 %collective-permute-start.5 = (f32[128,1]{1,0:T(8,128)S(1)}, f32[128,1]{1,0:T(8,128)S(1)}, u32[]{:S(2)}, u32[]{:S(2)}) collective-permute-start(f32[128,1]{1,0:T(8,128)S(1)} %get-tuple-element.2143), channel_id=1, source_target_pairs={{0,1},{1,2},{2,3},{3,4},{4,5},{5,6},{6,7},{8,9},{9,10},{10,11},{11... | collective-permute-start | bytes 1544 | tf_op jit(solution)/shard_map/ppermute | solution.py:24
  12.3 0.7 copy-start.4
  13.3 0.8 copy-start
  14.2 20.5 %collective-permute-start.2 = (f32[130,1]{1,0:T(8,128)S(1)}, f32[130,1]{1,0:T(8,128)S(1)}, u32[]{:S(2)}, u32[]{:S(2)}) collective-permute-start(f32[130,1]{1,0:T(8,128)S(1)} %get-tuple-element.2125), channel_id=1, source_target_pairs={{0,1},{1,2},{2,3},{3,4},{4,5},{5,6},{6,7},{8,9},{9,10},{10,11},{11... | collective-permute-start | bytes 1568 | tf_op jit(solution)/shard_map/ppermute | solution.py:24
  17.3 17.4 %collective-permute-start.3 = (f32[130,1]{1,0:T(8,128)S(1)}, f32[130,1]{1,0:T(8,128)S(1)}, u32[]{:S(2)}, u32[]{:S(2)}) collective-permute-start(f32[130,1]{1,0:T(8,128)S(1)} %get-tuple-element.2126), channel_id=1, source_target_pairs={{1,0},{2,1},{3,2},{4,3},{5,4},{6,5},{7,6},{9,8},{10,9},{11,10},{12... | collective-permute-start | bytes 1568 | tf_op jit(solution)/shard_map/ppermute | solution.py:25
  34.8 0.8 copy-start.1
  34.8 0.9 copy-start.2
  37.3 25.4 %all-to-all-start.3 = ((f32[128,8,16]{0,2,1:T(8,128)}), f32[128,8,16]{0,2,1:T(8,128)S(1)}, u32[]{:S(2)}, u32[]{:S(2)}) async-start(f32[128,8,16]{0,2,1:T(8,128)} %bitcast.82), calls=%async_computation.3 | async-start | bytes 131072 | tf_op jit(solution)/shard_map/all_to_all | solution.py:171
  62.7 11.0 %all-to-all-start.2 = ((f32[128,8,16]{0,2,1:T(8,128)}), f32[128,8,16]{0,2,1:T(8,128)S(1)}, u32[]{:S(2)}, u32[]{:S(2)}) async-start(f32[128,8,16]{0,2,1:T(8,128)} %bitcast.79), calls=%async_computation.2 | async-start | bytes 131072 | tf_op jit(solution)/shard_map/all_to_all | solution.py:170
  73.7 30.6 %all-to-all-start = ((f32[128,8,16]{0,2,1:T(8,128)}), f32[128,8,16]{0,2,1:T(8,128)S(1)}, u32[]{:S(2)}, u32[]{:S(2)}) async-start(f32[128,8,16]{0,2,1:T(8,128)} %bitcast.57), calls=%async_computation | async-start | bytes 131072 | tf_op jit(solution)/shard_map/all_to_all | solution.py:168
  102.6 0.7 copy-start.3
  104.3 11.0 %all-to-all-start.4 = ((f32[128,8,16]{0,2,1:T(8,128)}), f32[128,8,16]{0,2,1:T(8,128)S(1)}, u32[]{:S(2)}, u32[]{:S(2)}) async-start(f32[128,8,16]{0,2,1:T(8,128)} %bitcast.85), calls=%async_computation.4 | async-start | bytes 131072 | tf_op jit(solution)/shard_map/all_to_all | solution.py:169
  130.1 13.4 %collective-permute-start.6 = (f32[1,128]{1,0:T(1,128)S(1)}, f32[1,128]{1,0:T(1,128)S(1)}, u32[]{:S(2)}, u32[]{:S(2)}) collective-permute-start(f32[1,128]{1,0:T(1,128)S(1)} %get-tuple-element.2136), channel_id=1, source_target_pairs={{8,0},{16,8},{24,16},{9,1},{17,9},{25,17},{10,2},{18,10},{26,18},{... | collective-permute-start | bytes 1544 | tf_op jit(solution)/shard_map/ppermute | solution.py:25
  131.4 12.1 %collective-permute-start.7 = (f32[1,128]{1,0:T(1,128)S(1)}, f32[1,128]{1,0:T(1,128)S(1)}, u32[]{:S(2)}, u32[]{:S(2)}) collective-permute-start(f32[1,128]{1,0:T(1,128)S(1)} %get-tuple-element.2137), channel_id=1, source_target_pairs={{0,8},{8,16},{16,24},{1,9},{9,17},{17,25},{2,10},{10,18},{18,26},{... | collective-permute-start | bytes 1544 | tf_op jit(solution)/shard_map/ppermute | solution.py:24
  145.0 11.0 %all-to-all-start.1 = ((f32[128,8,16]{0,2,1:T(8,128)}), f32[128,8,16]{0,2,1:T(8,128)S(1)}, u32[]{:S(2)}, u32[]{:S(2)}) async-start(f32[128,8,16]{0,2,1:T(8,128)} %bitcast.76), calls=%async_computation.1 | async-start | bytes 131072 | tf_op jit(solution)/shard_map/all_to_all | solution.py:213
  179.7 10.9 %all-to-all-start.5 = ((f32[128,8,16]{0,2,1:T(8,128)}), f32[128,8,16]{0,2,1:T(8,128)S(1)}, u32[]{:S(2)}, u32[]{:S(2)}) async-start(f32[128,8,16]{0,2,1:T(8,128)} %bitcast.100), calls=%async_computation.5 | async-start | bytes 131072 | tf_op jit(solution)/shard_map/all_to_all | solution.py:235
  219.2 5.9 %collective-permute-start.8 = (f32[1,128]{1,0:T(1,128)S(1)}, f32[1,128]{1,0:T(1,128)S(1)}, u32[]{:S(2)}, u32[]{:S(2)}) collective-permute-start(f32[1,128]{1,0:T(1,128)S(1)} %get-tuple-element.2127), channel_id=1, source_target_pairs={{8,0},{16,8},{24,16},{9,1},{17,9},{25,17},{10,2},{18,10},{26,18},{... | collective-permute-start | bytes 1544 | tf_op jit(solution)/shard_map/ppermute | solution.py:25
  220.5 5.8 %collective-permute-start.9 = (f32[1,128]{1,0:T(1,128)S(1)}, f32[1,128]{1,0:T(1,128)S(1)}, u32[]{:S(2)}, u32[]{:S(2)}) collective-permute-start(f32[1,128]{1,0:T(1,128)S(1)} %get-tuple-element.2128), channel_id=1, source_target_pairs={{0,8},{8,16},{16,24},{1,9},{9,17},{17,25},{2,10},{10,18},{18,26},{... | collective-permute-start | bytes 1544 | tf_op jit(solution)/shard_map/ppermute | solution.py:24
  227.9 9.2 %all-to-all-start.6 = ((f32[128,8,16]{0,2,1:T(8,128)}), f32[128,8,16]{0,2,1:T(8,128)S(1)}, u32[]{:S(2)}, u32[]{:S(2)}) async-start(f32[128,8,16]{0,2,1:T(8,128)} %bitcast.112), calls=%async_computation.6 | async-start | bytes 131072 | tf_op jit(solution)/shard_map/all_to_all | solution.py:213
where the time goes:
time: 270 us; the launch traced here: 268 us
  local copies, waits for them, and re-layouts  74.3 us (28%)
  starting transfers between devices  57.8 us (21%)
  other arithmetic  44.2 us (16%)
  loops' own time  39.9 us (15%)
  blocking collectives  26.6 us (10%)
  waiting for transfers between devices  24.6 us (9%)
    dynamic_update_slice x1536, local copies, waits for them, and re-layouts, factor(): lax.scan(advance, jnp.zeros_like(main_diag[0]), (sub_diag, main_diag, sup...  57.8 us
    ppermute x5, starting transfers between devices, with_halo(): before = lax.ppermute(last, axis, up)  20.1 us
    all_gather x2, blocking collectives, local(): gathered = lax.all_gather(solve_own_rel[None], 'gx', axis=0, tiled=True)  18.4 us
    another operation x6, loops' own time, substitute(): lax.scan(forward, jnp.zeros_like(source[0]), (sub_diag, pivots, source))  16.7 us
    another operation x6, loops' own time, substitute(): lax.scan(backward, jnp.zeros_like(source[0]), (ratios, partial_sol), reve...  16.7 us
    mul x512, other arithmetic, forward(): new_value = (source_row - sub_row * prev_value) * pivot_row  10.2 us
    sub x512, other arithmetic, backward(): new_value = partial_row - ratio_row * next_value  9.7 us
    dynamic_update_slice x512, other arithmetic, substitute(): lax.scan(forward, jnp.zeros_like(source[0]), (sub_diag, pivots, source))  8.62 us

commit v1 on v0

v1 whole, which is shorter than its diff:
```python
import functools

import jax
import jax.numpy as jnp
from jax import lax
from jax.experimental import pallas as pl
from jax.experimental.pallas import tpu as pltpu
from jax.sharding import PartitionSpec as P

STEPS = 2
PITCH = 32
SUB = 8

xward_admittance = 1.0
yward_admittance = 0.5
warmth_scaling = 0.004
surrounding_warmth = 25.0
cushion_pieces = 1.0

MESH = pl.DeviceIdType.MESH


def roll(x, shift):
    return pltpu.roll(x, shift % x.shape[0], 0)


def sublanes(rows=SUB, lanes=128):
    return lax.broadcasted_iota(jnp.int32, (rows, lanes), 0)


def total(x):
    for step in (4, 2, 1):
        x = x + roll(x, step)
    return x


def wire(admittance, here, there):
    return admittance / (
        1.0 + warmth_scaling * (0.5 * (here + there) - surrounding_warmth)
    )


def pcr_factor(ground, link):
    rows = ground.shape[0]
    up = link
    down = jnp.where(sublanes(rows) == 0, 0.0, roll(link, 1))
    levels = []
    step = 1
    while step < rows:
        inverse = 1.0 / (ground + up + down)
        take_up = up * roll(inverse, -step)
        take_down = down * roll(inverse, step)
        levels.append((step, take_up, take_down))
        ground = ground + take_up * roll(ground, -step) + take_down * roll(ground, step)
        up, down = take_up * roll(up, -step), take_down * roll(down, step)
        step *= 2
    return levels, 1.0 / ground


def pcr_apply(factors, source):
    levels, inverse = factors
    for step, take_up, take_down in levels:
        source = source + take_up * roll(source, -step) + take_down * roll(source, step)
    return source * inverse


def chain_order(depth):
    order, step = [], 1
    while step < depth:
        order.append([(k, k - step, k + step) for k in range(step, depth, 2 * step)])
        step *= 2
    return order


def after(first, fill):
    return jnp.where(sublanes() == SUB - 1, fill, roll(first, -1))


class Line:
    def __init__(self, ground, link):
        depth = len(ground)
        self.depth = depth
        sub = sublanes()
        own = list(ground) + [jnp.zeros_like(ground[0])]
        right = list(link)
        self.node = {}
        for level in chain_order(depth):
            for k, lo, hi in level:
                left_link, right_link = right[lo], right[k]
                inverse = 1.0 / (own[k] + left_link + right_link)
                to_lo, to_hi = left_link * inverse, right_link * inverse
                self.node[k] = (inverse, to_lo, to_hi)
                own[lo] = own[lo] + to_lo * own[k]
                own[hi] = own[hi] + to_hi * own[k]
                right[lo] = to_lo * right_link
        joined = right[0]
        held = own[0] + jnp.where(sub == 0, 0.0, roll(own[depth], 1))
        inner = sub > 0
        first_link = jnp.where(sub == 1, roll(joined, 1), 0.0)
        last_link = jnp.where(sub == SUB - 1, joined, 0.0)
        held = jnp.where(inner, held + first_link + last_link, 1.0)
        between = jnp.where(inner & (sub < SUB - 1), joined, 0.0)
        self.heads = pcr_factor(held, between)
        near = jnp.where(inner, pcr_apply(self.heads, first_link), 1.0)
        far = jnp.where(inner, pcr_apply(self.heads, last_link), 0.0)
        self.near = self.fill(near, after(near, 0.0))
        self.far = self.fill(far, after(far, 1.0))
        first = sub == 0
        bridge = jnp.where(first, joined * roll(far, -1), 0.0)
        near_ground, far_ground = self.condense(ground)
        self.coefficients = jnp.where(
            first,
            total(near_ground),
            jnp.where(sub == 1, total(far_ground), jnp.where(sub == 2, roll(bridge, 2), 0.0)),
        )

    def fill(self, first, last, source=None):
        value = {0: first, self.depth: last}
        for level in reversed(chain_order(self.depth)):
            for k, lo, hi in level:
                inverse, to_lo, to_hi = self.node[k]
                out = to_lo * value[lo] + to_hi * value[hi]
                value[k] = out if source is None else source[k] * inverse + out
        return [value[k] for k in range(self.depth)]

    def condense(self, source):
        near = [a * b for a, b in zip(self.near, source)]
        far = [a * b for a, b in zip(self.far, source)]
        while len(near) > 1:
            near = [a + b for a, b in zip(near[::2], near[1::2])]
            far = [a + b for a, b in zip(far[::2], far[1::2])]
        return near[0], far[0]

    def message(self, source):
        near, far = self.condense(source)
        return jnp.where(sublanes() < 4, near + roll(near, 4), far + roll(far, 4))

    def inside(self, source):
        sub = sublanes()
        now = list(source) + [jnp.zeros_like(source[0])]
        for level in chain_order(self.depth):
            for k, lo, hi in level:
                _, to_lo, to_hi = self.node[k]
                now[lo] = now[lo] + to_lo * now[k]
                now[hi] = now[hi] + to_hi * now[k]
        head = jnp.where(sub == 0, 0.0, now[0] + roll(now[self.depth], 1))
        first = pcr_apply(self.heads, head)
        return self.fill(first, after(first, 0.0), now)

    def weigh(self, parts, place):
        devices = len(parts)
        rows = max(SUB, devices)
        at = sublanes(rows)
        spread = [jnp.zeros((rows, 128), jnp.float32) for _ in range(3)]
        for d, part in enumerate(parts):
            for r in range(3):
                spread[r] = jnp.where(at == d, part[r : r + 1], spread[r])
        ground = spread[0] + roll(spread[1], 1)
        ground = jnp.where(at < devices, ground, 1.0)
        factors = pcr_factor(ground, spread[2])
        upper = sublanes() < 4
        blank = jnp.zeros((1, 128), jnp.float32)
        self.weights = []
        for kept in (place, place + 1):
            unit = jnp.where((at == kept) & (at < devices), 1.0, 0.0)
            row = pcr_apply(factors, unit)
            self.weights.append(
                [
                    jnp.where(upper, row[d : d + 1], row[d + 1 : d + 2] if d + 1 < devices else blank)
                    for d in range(devices)
                ]
            )

    def finish(self, messages, inside):
        own, next_one = (
            total(functools.reduce(jnp.add, [w * m for w, m in zip(weights, messages)]))
            for weights in self.weights
        )
        return [
            u + near * own + far * next_one
            for u, near, far in zip(inside, self.near, self.far)
        ]


class Exchange:
    def __init__(self, axis, devices, mine, slots, send_sem, recv_sem):
        place = lax.axis_index(axis)
        self.copies = [
            pltpu.make_async_remote_copy(
                src_ref=mine,
                dst_ref=slots.at[place],
                send_sem=send_sem.at[ahead - 1],
                recv_sem=recv_sem.at[ahead - 1],
                device_id={axis: lax.rem(place + ahead, devices)},
                device_id_type=MESH,
            )
            for ahead in range(1, devices)
        ]
        self.place, self.devices, self.mine, self.slots = place, devices, mine, slots

    def start(self, value):
        self.mine[...] = value
        for copy in self.copies:
            copy.start()

    def arrived(self):
        for copy in self.copies:
            copy.wait_recv()
        return [
            jnp.where(self.place == d, self.mine[...], self.slots[d]) for d in range(self.devices)
        ]

    def close(self):
        for copy in self.copies:
            copy.wait_send()


def kernel(
    count_x, count_y,
    sag_ref, warmth_ref, store_ref, load_ref, flag_ref,
    out_ref,
    turn_ref, halo_x, halo_y, edge_y,
    mine_x0, slots_x0, mine_x1, slots_x1,
    mine_yc, slots_yc, mine_y0, slots_y0, mine_y1, slots_y1,
    halo_send, halo_recv,
    x0_send, x0_recv, x1_send, x1_recv,
    yc_send, yc_recv, y0_send, y0_recv, y1_send, y1_recv,
):
    place_x = lax.axis_index("gx")
    place_y = lax.axis_index("gy")
    rows, cols = sag_ref.shape
    depth_x, depth_y = rows // SUB, cols // SUB
    sub = sublanes()
    lane = lax.broadcasted_iota(jnp.int32, (SUB, 128), 1)

    halo_x[...] = jnp.zeros_like(halo_x)
    halo_y[...] = jnp.zeros_like(halo_y)
    barrier = pltpu.get_barrier_semaphore()
    for axis, place, devices in (("gx", place_x, count_x), ("gy", place_y, count_y)):
        for ahead in range(1, devices):
            pl.semaphore_signal(
                barrier, inc=1,
                device_id={axis: lax.rem(place + ahead, devices)}, device_id_type=MESH,
            )

    def split(ref, depth):
        return [ref[pl.ds(k, SUB, stride=depth), :] for k in range(depth)]

    def to_y(parts):
        turn_ref[...] = jnp.concatenate(parts, 0).T
        return split(turn_ref, depth_y)

    def to_x(parts):
        for k, part in enumerate(parts):
            turn_ref[pl.ds(k, SUB, stride=depth_y), :] = part
        turned = turn_ref[...].T
        return [turned[SUB * k : SUB * k + SUB] for k in range(depth_x)]

    warmth_x = split(warmth_ref, depth_x)
    warmth_y = to_y(warmth_x)
    sag_y = to_y(split(sag_ref, depth_x))
    end_y = depth_y - 1
    edge_y[0] = jnp.where(sub == 0, warmth_y[0], roll(sag_y[0], 1))
    edge_y[1] = jnp.where(sub == 0, roll(warmth_y[end_y], 1), roll(sag_y[end_y], 2))

    pl.semaphore_wait(barrier, count_x - 1 + count_y - 1)

    halos = [
        (place_x > 0, place_x < count_x - 1, pltpu.make_async_remote_copy(
            src_ref=warmth_ref.at[pl.ds(0, SUB)], dst_ref=halo_x,
            send_sem=halo_send.at[0], recv_sem=halo_recv.at[0],
            device_id={"gx": lax.rem(place_x + count_x - 1, count_x)}, device_id_type=MESH)),
        (place_y > 0, place_y < count_y - 1, pltpu.make_async_remote_copy(
            src_ref=edge_y.at[0], dst_ref=halo_y.at[0],
            send_sem=halo_send.at[1], recv_sem=halo_recv.at[1],
            device_id={"gy": lax.rem(place_y + count_y - 1, count_y)}, device_id_type=MESH)),
        (place_y < count_y - 1, place_y > 0, pltpu.make_async_remote_copy(
            src_ref=edge_y.at[1], dst_ref=halo_y.at[1],
            send_sem=halo_send.at[2], recv_sem=halo_recv.at[2],
            device_id={"gy": lax.rem(place_y + 1, count_y)}, device_id_type=MESH)),
    ]
    for sends, _, copy in halos:
        pl.when(sends)(copy.start)

    store_x = split(store_ref, depth_x)
    store_y = to_y(store_x)
    cushion_x = jnp.zeros((SUB, 128), jnp.float32)
    cushion_y = jnp.zeros((SUB, 128), jnp.float32)
    for a in range(rows // PITCH):
        for b in range(cols // PITCH):
            flag = cushion_pieces * flag_ref[a, b].astype(jnp.float32)
            at_a, at_b = PITCH // depth_x * a, PITCH // depth_y * b
            cushion_x = jnp.where((sub == at_a) & (lane == PITCH * b), flag, cushion_x)
            cushion_y = jnp.where((sub == at_b) & (lane == at_a), flag, cushion_y)
    ground_x = [store_x[0] + cushion_x] + store_x[1:]
    ground_y = [store_y[0] + cushion_y] + store_y[1:]

    for _, receives, copy in halos:
        pl.when(receives)(copy.wait_recv)

    last_x = (sub == SUB - 1) & (place_x == count_x - 1)
    last_y = (sub == SUB - 1) & (place_y == count_y - 1)
    first_y = (sub == 0) & (place_y == 0)
    next_x = warmth_x[1:] + [after(warmth_x[0], halo_x[0:1])]
    link_x = [wire(xward_admittance, a, b) for a, b in zip(warmth_x, next_x)]
    link_x[-1] = jnp.where(last_x, 0.0, link_x[-1])
    next_y = warmth_y[1:] + [after(warmth_y[0], halo_y[0, 0:1])]
    link_y = [wire(yward_admittance, a, b) for a, b in zip(warmth_y, next_y)]
    link_y[-1] = jnp.where(last_y, 0.0, link_y[-1])

    next_sag = sag_y[1:] + [after(sag_y[0], halo_y[0, 1:2])]
    flow = [g * (a - b) for g, a, b in zip(link_y, sag_y, next_sag)]
    inflow = wire(yward_admittance, halo_y[1, 0:1], warmth_y[0]) * (halo_y[1, 1:2] - sag_y[0])
    inflow = jnp.where(first_y, 0.0, inflow)
    flow_in = [jnp.where(sub == 0, inflow, roll(flow[-1], 1))] + flow[:-1]
    source_y = [c * v - (o - i) for c, v, o, i in zip(store_y, sag_y, flow, flow_in)]
    source_y[0] = source_y[0] - cushion_y * sag_y[0]

    exchange_x = [
        Exchange("gx", count_x, mine_x0, slots_x0, x0_send, x0_recv),
        Exchange("gx", count_x, mine_x1, slots_x1, x1_send, x1_recv),
    ]
    share_y = Exchange("gy", count_y, mine_yc, slots_yc, yc_send, yc_recv)
    exchange_y = [
        Exchange("gy", count_y, mine_y0, slots_y0, y0_send, y0_recv),
        Exchange("gy", count_y, mine_y1, slots_y1, y1_send, y1_recv),
    ]

    line_x = Line(ground_x, link_x)
    load = [split(load_ref.at[s], depth_x) for s in range(STEPS)]
    source = [a + b for a, b in zip(to_x(source_y), load[0])]
    for s in range(STEPS):
        message = line_x.message(source)
        if s == 0:
            exchange_x[s].start(jnp.stack([message, line_x.coefficients]))
            line_y = Line(ground_y, link_y)
            share_y.start(line_y.coefficients)
        else:
            exchange_x[s].start(message)
        inside = line_x.inside(source)
        got = exchange_x[s].arrived()
        if s == 0:
            line_x.weigh([part[1] for part in got], place_x)
            got = [part[0] for part in got]
        half = line_x.finish(got, inside)
        source = [2.0 * c * h - f + q for c, h, f, q in zip(store_x, half, source, load[s])]
        source_y = to_y(source)
        exchange_y[s].start(line_y.message(source_y))
        if s == 0:
            line_y.weigh(share_y.arrived(), place_y)
        inside = line_y.inside(source_y)
        drop = line_y.finish(exchange_y[s].arrived(), inside)
        if s + 1 < STEPS:
            carried = [2.0 * c * v - f for c, v, f in zip(store_y, drop, source_y)]
            source = [a + b for a, b in zip(to_x(carried), load[s + 1])]
    for k, part in enumerate(to_x(drop)):
        out_ref[pl.ds(k, SUB, stride=depth_x), :] = part

    for exchange in exchange_x + [share_y] + exchange_y:
        exchange.close()
    for sends, _, copy in halos:
        pl.when(sends)(copy.wait_send)


def local(count_x, count_y, sag, warmth, store, load, flags):
    tile = (SUB, 128)
    vmem = pl.BlockSpec(memory_space=pltpu.VMEM)

    def buffers(devices, shape):
        return [pltpu.VMEM(shape, jnp.float32), pltpu.VMEM((devices,) + shape, jnp.float32)]

    def semaphores(devices):
        return [pltpu.SemaphoreType.DMA((devices - 1,))] * 2

    return pl.pallas_call(
        functools.partial(kernel, count_x, count_y),
        out_shape=jax.ShapeDtypeStruct(sag.shape, jnp.float32),
        in_specs=[vmem] * 4 + [pl.BlockSpec(memory_space=pltpu.SMEM)],
        out_specs=vmem,
        scratch_shapes=[
            pltpu.VMEM((sag.shape[1], sag.shape[0]), jnp.float32),
            pltpu.VMEM(tile, jnp.float32),
            pltpu.VMEM((2,) + tile, jnp.float32),
            pltpu.VMEM((2,) + tile, jnp.float32),
            *buffers(count_x, (2,) + tile),
            *buffers(count_x, tile),
            *buffers(count_y, tile),
            *buffers(count_y, tile),
            *buffers(count_y, tile),
            pltpu.SemaphoreType.DMA((3,)),
            pltpu.SemaphoreType.DMA((3,)),
            *semaphores(count_x),
            *semaphores(count_x),
            *semaphores(count_y),
            *semaphores(count_y),
            *semaphores(count_y),
        ],
        compiler_params=pltpu.CompilerParams(
            collective_id=0, has_side_effects=True, vmem_limit_bytes=16 * 2**20
        ),
    )(sag, warmth, store, load, flags)


def solution(mesh):
    return jax.shard_map(
        functools.partial(local, mesh.shape["gx"], mesh.shape["gy"]),
        mesh=mesh,
        in_specs=(P("gx", "gy"), P("gx", "gy"), P("gx", "gy"), P(None, "gx", "gy"), P("gx", "gy")),
        out_specs=P("gx", "gy"),
        check_vma=False,
    )
```

time: 270 us -> 28.7 us (0.11)
  local copies, waits for them, and re-layouts: 74.3 us -> 4.73 us
  starting transfers between devices: 57.8 us -> 0 us
  other arithmetic: 44.2 us -> 0 us
  loops' own time: 39.9 us -> 0 us
  blocking collectives: 26.6 us -> 0 us
  waiting for transfers between devices: 24.6 us -> 0 us
  Pallas kernels: 0 us -> 23.7 us
    dynamic_update_slice x1584 -> x0, local copies, waits for them, and re-layouts: 58.2 us -> none  [the longest x1536 57.8 us: factor(): lax.scan(advance, jnp.zeros_like(main_diag[0]), (sub_diag, main_diag, sup...]
    another operation x22 -> x0, loops' own time: 39.9 us -> none  [the longest x6 16.7 us: substitute(): lax.scan(forward, jnp.zeros_like(source[0]), (sub_diag, pivots, source))]
    all_to_all x7 -> x0, starting transfers between devices: 31.3 us -> none  [the longest x2 6.7 us: local(): lax.all_to_all(source.T, 'gy', split_axis=1, concat_axis=1, tiled=True)]
    ppermute x10 -> x0, starting transfers between devices: 26.5 us -> none  [the longest x5 20.1 us: with_halo(): before = lax.ppermute(last, axis, up)]
    pallas_call x0 -> x1, Pallas kernels: none -> 23.7 us  [local(): pl.pallas_call(functools.partial(kernel, count_x, count_y), out_shape=jax...]
    all_to_all x7 -> x0, waiting for transfers between devices: 23.3 us -> none  [the longest x1 5.91 us: local(): lax.all_to_all(payload, 'gy', split_axis=1, concat_axis=1, tiled=True)]
    all_gather x2 -> x0, blocking collectives: 18.4 us -> none  [local(): gathered = lax.all_gather(solve_own_rel[None], 'gx', axis=0, tiled=True)]
    mul x839 -> x0, other arithmetic: 16.6 us -> none  [the longest x512 10.2 us: forward(): new_value = (source_row - sub_row * prev_value) * pivot_row]
where the time goes in v1:
time: 28.7 us; the launch traced here: 28.4 us
  Pallas kernels  23.7 us (83%)
  local copies, waits for them, and re-layouts  4.73 us (16%)
    pallas_call x1, Pallas kernels, local(): pl.pallas_call(functools.partial(kernel, count_x, count_y), out_shape=jax...  23.7 us
    unnamed x11, local copies, waits for them, and re-layouts  4.73 us

profile of v1, /device:TPU:0, one launch (start us, length us, event | category | flops | bytes accessed | tf_op | source)
XLA Modules:
  0.0 28.4 jit_solution(7317728752464499386)
XLA Ops:
  0.0 0.0 copy-start
  0.0 0.9 %copy-done = f32[2,128,128]{2,1,0:T(8,128)S(1)} copy-done((f32[2,128,128]{2,1,0:T(8,128)S(1)}, f32[2,128,128]{2,1,0:T(8,128)}, u32[]{:S(2)}) %copy-start) | copy-done | bytes 131096
  0.9 0.0 copy-start.1
  0.9 0.8 %copy-done.1 = f32[128,128]{1,0:T(8,128)S(1)} copy-done((f32[128,128]{1,0:T(8,128)S(1)}, f32[128,128]{1,0:T(8,128)}, u32[]{:S(2)}) %copy-start.1) | copy-done | bytes 65560
  1.7 0.0 copy-start.2
  1.7 0.8 %copy-done.2 = f32[128,128]{1,0:T(8,128)S(1)} copy-done((f32[128,128]{1,0:T(8,128)S(1)}, f32[128,128]{1,0:T(8,128)}, u32[]{:S(2)}) %copy-start.2) | copy-done | bytes 65560
  2.6 0.0 copy-start.3
  2.6 0.8 %copy-done.3 = f32[128,128]{1,0:T(8,128)S(1)} copy-done((f32[128,128]{1,0:T(8,128)S(1)}, f32[128,128]{1,0:T(8,128)}, u32[]{:S(2)}) %copy-start.3) | copy-done | bytes 65560
  3.4 0.0 copy-start.4
  3.4 0.7 %copy-done.4 = s32[4,4]{1,0:T(4,128)S(1)} copy-done((s32[4,4]{1,0:T(4,128)S(1)}, s32[4,4]{1,0:T(4,128)}, u32[]{:S(2)}) %copy-start.4) | copy-done | bytes 88
  4.1 23.7 %shard_map.55 = f32[128,128]{1,0:T(8,128)S(1)} custom-call(f32[128,128]{1,0:T(8,128)S(1)} %copy-done.1, f32[128,128]{1,0:T(8,128)S(1)} %copy-done.2, f32[128,128]{1,0:T(8,128)S(1)} %copy-done.3, f32[2,128,128]{2,1,0:T(8,128)S(1)} %copy-done, s32[4,4]{1,0:T(4,128)S(1)} %copy-done.4), custom_call_target="tpu_custom_call" | custom-call | tf_op jit(solution)/shard_map/pallas_call | solution.py:375
  27.8 0.6 %copy.7 = f32[128,128]{1,0:T(8,128)} copy(f32[128,128]{1,0:T(8,128)S(1)} %shard_map.55) | data formatting | bytes 131072
Async XLA Ops:
  0.0 0.9 %copy-start = (f32[2,128,128]{2,1,0:T(8,128)S(1)}, f32[2,128,128]{2,1,0:T(8,128)}, u32[]{:S(2)}) copy-start(f32[2,128,128]{2,1,0:T(8,128)} %load_ref.1) | copy-start | bytes 393220
  0.9 0.8 %copy-start.1 = (f32[128,128]{1,0:T(8,128)S(1)}, f32[128,128]{1,0:T(8,128)}, u32[]{:S(2)}) copy-start(f32[128,128]{1,0:T(8,128)} %sag_ref.1) | copy-start | bytes 196612
  1.7 0.8 %copy-start.2 = (f32[128,128]{1,0:T(8,128)S(1)}, f32[128,128]{1,0:T(8,128)}, u32[]{:S(2)}) copy-start(f32[128,128]{1,0:T(8,128)} %warmth_ref.1) | copy-start | bytes 196612
  2.6 0.8 %copy-start.3 = (f32[128,128]{1,0:T(8,128)S(1)}, f32[128,128]{1,0:T(8,128)}, u32[]{:S(2)}) copy-start(f32[128,128]{1,0:T(8,128)} %store_ref.1) | copy-start | bytes 196612
  3.4 0.7 %copy-start.4 = (s32[4,4]{1,0:T(4,128)S(1)}, s32[4,4]{1,0:T(4,128)}, u32[]{:S(2)}) copy-start(s32[4,4]{1,0:T(4,128)} %flag_ref.1) | copy-start | bytes 196

commit v2 on v1

--- a/solution.py
+++ b/solution.py
@@ -10,6 +10,7 @@
 STEPS = 2
 PITCH = 32
 SUB = 8
+SHORT = 1e20
 
 xward_admittance = 1.0
 yward_admittance = 0.5
@@ -77,12 +78,14 @@
 
 
 class Line:
-    def __init__(self, ground, link):
+    def __init__(self, ground, link, warmth, admittance):
         depth = len(ground)
         self.depth = depth
         sub = sublanes()
         own = list(ground) + [jnp.zeros_like(ground[0])]
         right = list(link)
+        right[-1] = jnp.where(sub == SUB - 1, SHORT, right[-1])
+        self.admittance = admittance
         self.node = {}
         for level in chain_order(depth):
             for k, lo, hi in level:
@@ -108,11 +111,11 @@
         first = sub == 0
         bridge = jnp.where(first, joined * roll(far, -1), 0.0)
         near_ground, far_ground = self.condense(ground)
-        self.coefficients = jnp.where(
-            first,
-            total(near_ground),
-            jnp.where(sub == 1, total(far_ground), jnp.where(sub == 2, roll(bridge, 2), 0.0)),
-        )
+        rows = [total(near_ground), total(far_ground), roll(bridge, 2)]
+        rows += [roll(warmth[0], 3), roll(warmth[-1], 5)]
+        self.coefficients = jnp.zeros_like(ground[0])
+        for r, row in enumerate(rows):
+            self.coefficients = jnp.where(sub == r, row, self.coefficients)
 
     def fill(self, first, last, source=None):
         value = {0: first, self.depth: last}
@@ -149,35 +152,36 @@
 
     def weigh(self, parts, place):
         devices = len(parts)
-        rows = max(SUB, devices)
+        rows = max(SUB, 2 * devices)
         at = sublanes(rows)
-        spread = [jnp.zeros((rows, 128), jnp.float32) for _ in range(3)]
+        ground = jnp.ones((rows, 128), jnp.float32)
+        link = jnp.zeros((rows, 128), jnp.float32)
         for d, part in enumerate(parts):
-            for r in range(3):
-                spread[r] = jnp.where(at == d, part[r : r + 1], spread[r])
-        ground = spread[0] + roll(spread[1], 1)
-        ground = jnp.where(at < devices, ground, 1.0)
-        factors = pcr_factor(ground, spread[2])
+            ground = jnp.where(at == 2 * d, part[0:1], ground)
+            ground = jnp.where(at == 2 * d + 1, part[1:2], ground)
+            link = jnp.where(at == 2 * d, part[2:3], link)
+            if d + 1 < devices:
+                between = wire(self.admittance, part[4:5], parts[d + 1][3:4])
+                link = jnp.where(at == 2 * d + 1, between, link)
+        factors = pcr_factor(ground, link)
         upper = sublanes() < 4
-        blank = jnp.zeros((1, 128), jnp.float32)
         self.weights = []
-        for kept in (place, place + 1):
-            unit = jnp.where((at == kept) & (at < devices), 1.0, 0.0)
-            row = pcr_apply(factors, unit)
+        for kept in (2 * place, 2 * place + 1):
+            row = pcr_apply(factors, jnp.where(at == kept, 1.0, 0.0))
             self.weights.append(
                 [
-                    jnp.where(upper, row[d : d + 1], row[d + 1 : d + 2] if d + 1 < devices else blank)
+                    jnp.where(upper, row[2 * d : 2 * d + 1], row[2 * d + 1 : 2 * d + 2])
                     for d in range(devices)
                 ]
             )
 
     def finish(self, messages, inside):
-        own, next_one = (
+        first, last = (
             total(functools.reduce(jnp.add, [w * m for w, m in zip(weights, messages)]))
             for weights in self.weights
         )
         return [
-            u + near * own + far * next_one
+            u + near * first + far * last
             for u, near, far in zip(inside, self.near, self.far)
         ]
 
@@ -194,7 +198,7 @@
                 device_id={axis: lax.rem(place + ahead, devices)},
                 device_id_type=MESH,
             )
-            for ahead in range(1, devices)
+            for ahead in sorted(range(1, devices), key=lambda a: -min(a, devices - a))
         ]
         self.place, self.devices, self.mine, self.slots = place, devices, mine, slots
 
@@ -217,13 +221,14 @@
 
 def kernel(
     count_x, count_y,
-    sag_ref, warmth_ref, store_ref, load_ref, flag_ref,
+    sag_hbm, warmth_hbm, store_hbm, load_hbm, flag_hbm,
     out_ref,
-    turn_ref, halo_x, halo_y, edge_y,
-    mine_x0, slots_x0, mine_x1, slots_x1,
+    sag_ref, warmth_ref, store_ref, load_ref, flag_ref, fetch_sem,
+    turn_ref, halo_y, edge_y,
+    mine_xc, slots_xc, mine_x0, slots_x0, mine_x1, slots_x1,
     mine_yc, slots_yc, mine_y0, slots_y0, mine_y1, slots_y1,
     halo_send, halo_recv,
-    x0_send, x0_recv, x1_send, x1_recv,
+    xc_send, xc_recv, x0_send, x0_recv, x1_send, x1_recv,
     yc_send, yc_recv, y0_send, y0_recv, y1_send, y1_recv,
 ):
     place_x = lax.axis_index("gx")
@@ -233,7 +238,15 @@
     sub = sublanes()
     lane = lax.broadcasted_iota(jnp.int32, (SUB, 128), 1)
 
-    halo_x[...] = jnp.zeros_like(halo_x)
+    fetches = [
+        pltpu.make_async_copy(src, dst, fetch_sem.at[k])
+        for k, (src, dst) in enumerate([
+            (warmth_hbm, warmth_ref), (sag_hbm, sag_ref), (store_hbm, store_ref),
+            (flag_hbm, flag_ref), (load_hbm, load_ref),
+        ])
+    ]
+    for fetch in fetches:
+        fetch.start()
     halo_y[...] = jnp.zeros_like(halo_y)
     barrier = pltpu.get_barrier_semaphore()
     for axis, place, devices in (("gx", place_x, count_x), ("gy", place_y, count_y)):
@@ -256,6 +269,8 @@
         turned = turn_ref[...].T
         return [turned[SUB * k : SUB * k + SUB] for k in range(depth_x)]
 
+    fetches[0].wait()
+    fetches[1].wait()
     warmth_x = split(warmth_ref, depth_x)
     warmth_y = to_y(warmth_x)
     sag_y = to_y(split(sag_ref, depth_x))
@@ -266,22 +281,20 @@
     pl.semaphore_wait(barrier, count_x - 1 + count_y - 1)
 
     halos = [
-        (place_x > 0, place_x < count_x - 1, pltpu.make_async_remote_copy(
-            src_ref=warmth_ref.at[pl.ds(0, SUB)], dst_ref=halo_x,
-            send_sem=halo_send.at[0], recv_sem=halo_recv.at[0],
-            device_id={"gx": lax.rem(place_x + count_x - 1, count_x)}, device_id_type=MESH)),
         (place_y > 0, place_y < count_y - 1, pltpu.make_async_remote_copy(
             src_ref=edge_y.at[0], dst_ref=halo_y.at[0],
-            send_sem=halo_send.at[1], recv_sem=halo_recv.at[1],
+            send_sem=halo_send.at[0], recv_sem=halo_recv.at[0],
             device_id={"gy": lax.rem(place_y + count_y - 1, count_y)}, device_id_type=MESH)),
         (place_y < count_y - 1, place_y > 0, pltpu.make_async_remote_copy(
             src_ref=edge_y.at[1], dst_ref=halo_y.at[1],
-            send_sem=halo_send.at[2], recv_sem=halo_recv.at[2],
+            send_sem=halo_send.at[1], recv_sem=halo_recv.at[1],
             device_id={"gy": lax.rem(place_y + 1, count_y)}, device_id_type=MESH)),
     ]
     for sends, _, copy in halos:
         pl.when(sends)(copy.start)
 
+    fetches[2].wait()
+    fetches[3].wait()
     store_x = split(store_ref, depth_x)
     store_y = to_y(store_x)
     cushion_x = jnp.zeros((SUB, 128), jnp.float32)
@@ -295,19 +308,20 @@
     ground_x = [store_x[0] + cushion_x] + store_x[1:]
     ground_y = [store_y[0] + cushion_y] + store_y[1:]
 
+    next_x = warmth_x[1:] + [roll(warmth_x[0], -1)]
+    link_x = [wire(xward_admittance, a, b) for a, b in zip(warmth_x, next_x)]
+    line_x = Line(ground_x, link_x, warmth_x, xward_admittance)
+    share_x = Exchange("gx", count_x, mine_xc, slots_xc, xc_send, xc_recv)
+    share_x.start(line_x.coefficients)
+
     for _, receives, copy in halos:
         pl.when(receives)(copy.wait_recv)
 
-    last_x = (sub == SUB - 1) & (place_x == count_x - 1)
     last_y = (sub == SUB - 1) & (place_y == count_y - 1)
     first_y = (sub == 0) & (place_y == 0)
-    next_x = warmth_x[1:] + [after(warmth_x[0], halo_x[0:1])]
-    link_x = [wire(xward_admittance, a, b) for a, b in zip(warmth_x, next_x)]
-    link_x[-1] = jnp.where(last_x, 0.0, link_x[-1])
     next_y = warmth_y[1:] + [after(warmth_y[0], halo_y[0, 0:1])]
     link_y = [wire(yward_admittance, a, b) for a, b in zip(warmth_y, next_y)]
     link_y[-1] = jnp.where(last_y, 0.0, link_y[-1])
-
     next_sag = sag_y[1:] + [after(sag_y[0], halo_y[0, 1:2])]
     flow = [g * (a - b) for g, a, b in zip(link_y, sag_y, next_sag)]
     inflow = wire(yward_admittance, halo_y[1, 0:1], warmth_y[0]) * (halo_y[1, 1:2] - sag_y[0])
@@ -326,23 +340,17 @@
         Exchange("gy", count_y, mine_y1, slots_y1, y1_send, y1_recv),
     ]
 
-    line_x = Line(ground_x, link_x)
+    fetches[4].wait()
     load = [split(load_ref.at[s], depth_x) for s in range(STEPS)]
     source = [a + b for a, b in zip(to_x(source_y), load[0])]
     for s in range(STEPS):
-        message = line_x.message(source)
+        exchange_x[s].start(line_x.message(source))
         if s == 0:
-            exchange_x[s].start(jnp.stack([message, line_x.coefficients]))
-            line_y = Line(ground_y, link_y)
+            line_x.weigh(share_x.arrived(), place_x)
+            line_y = Line(ground_y, link_y, warmth_y, yward_admittance)
             share_y.start(line_y.coefficients)
-        else:
-            exchange_x[s].start(message)
         inside = line_x.inside(source)
-        got = exchange_x[s].arrived()
-        if s == 0:
-            line_x.weigh([part[1] for part in got], place_x)
-            got = [part[0] for part in got]
-        half = line_x.finish(got, inside)
+        half = line_x.finish(exchange_x[s].arrived(), inside)
         source = [2.0 * c * h - f + q for c, h, f, q in zip(store_x, half, source, load[s])]
         source_y = to_y(source)
         exchange_y[s].start(line_y.message(source_y))
@@ -356,7 +364,7 @@
     for k, part in enumerate(to_x(drop)):
         out_ref[pl.ds(k, SUB, stride=depth_x), :] = part
 
-    for exchange in exchange_x + [share_y] + exchange_y:
+    for exchange in exchange_x + [share_x, share_y] + exchange_y:
         exchange.close()
     for sends, _, copy in halos:
         pl.when(sends)(copy.wait_send)
@@ -374,21 +382,25 @@
 
     return pl.pallas_call(
         functools.partial(kernel, count_x, count_y),
-        out_shape=jax.ShapeDtypeStruct(sag.shape, jnp.float32),
-        in_specs=[vmem] * 4 + [pl.BlockSpec(memory_space=pltpu.SMEM)],
+        out_shape=pltpu.VMEM(sag.shape, jnp.float32),
+        in_specs=[pl.BlockSpec(memory_space=pltpu.HBM)] * 5,
         out_specs=vmem,
         scratch_shapes=[
+            *(pltpu.VMEM(x.shape, jnp.float32) for x in (sag, warmth, store, load)),
+            pltpu.SMEM(flags.shape, jnp.int32),
+            pltpu.SemaphoreType.DMA((5,)),
             pltpu.VMEM((sag.shape[1], sag.shape[0]), jnp.float32),
-            pltpu.VMEM(tile, jnp.float32),
             pltpu.VMEM((2,) + tile, jnp.float32),
             pltpu.VMEM((2,) + tile, jnp.float32),
-            *buffers(count_x, (2,) + tile),
+            *buffers(count_x, tile),
+            *buffers(count_x, tile),
             *buffers(count_x, tile),
             *buffers(count_y, tile),
             *buffers(count_y, tile),
             *buffers(count_y, tile),
-            pltpu.SemaphoreType.DMA((3,)),
-            pltpu.SemaphoreType.DMA((3,)),
+            pltpu.SemaphoreType.DMA((2,)),
+            pltpu.SemaphoreType.DMA((2,)),
+            *semaphores(count_x),
             *semaphores(count_x),
             *semaphores(count_x),
             *semaphores(count_y),
@@ -398,7 +410,7 @@
         compiler_params=pltpu.CompilerParams(
             collective_id=0, has_side_effects=True, vmem_limit_bytes=16 * 2**20
         ),
-    )(sag, warmth, store, load, flags)
+    )(*(pltpu.with_memory_space_constraint(x, pltpu.HBM) for x in (sag, warmth, store, load, flags)))
 
 
 def solution(mesh):

time: 28.7 us -> 22.3 us (0.78)
  local copies, waits for them, and re-layouts: 4.73 us -> 0.63 us
  Pallas kernels: 23.7 us -> 21.5 us
    unnamed x11 -> x1, local copies, waits for them, and re-layouts: 4.73 us -> 0.63 us
    pallas_call x1, Pallas kernels: 23.7 us -> 21.5 us  [local(): pl.pallas_call(functools.partial(kernel, count_x, count_y), out_shape=plt...]
where the time goes in v2:
time: 22.3 us; the launch traced here: 22.1 us
  Pallas kernels  21.5 us (96%)
  local copies, waits for them, and re-layouts  0.63 us (3%)
    pallas_call x1, Pallas kernels, local(): pl.pallas_call(functools.partial(kernel, count_x, count_y), out_shape=plt...  21.5 us
    unnamed x1, local copies, waits for them, and re-layouts  0.63 us

profile of v2, /device:TPU:0, one launch (start us, length us, event | category | flops | bytes accessed | tf_op | source)
XLA Modules:
  0.0 22.1 jit_solution(9769969386323983286)
XLA Ops:
  0.0 21.5 %shard_map.55 = f32[128,128]{1,0:T(8,128)S(1)} custom-call(f32[128,128]{1,0:T(8,128)} %sag_hbm.1, f32[128,128]{1,0:T(8,128)} %warmth_hbm.1, f32[128,128]{1,0:T(8,128)} %store_hbm.1, f32[2,128,128]{2,1,0:T(8,128)} %load_hbm.1, s32[4,4]{1,0:T(4,128)} %flag_hbm.1), custom_call_target="tpu_custom_call" | custom-call | tf_op jit(solution)/shard_map/pallas_call | solution.py:383
  21.5 0.6 %copy.7 = f32[128,128]{1,0:T(8,128)} copy(f32[128,128]{1,0:T(8,128)S(1)} %shard_map.55) | data formatting | bytes 131072

commit v3 on v2

--- a/solution.py
+++ b/solution.py
@@ -33,6 +33,10 @@
     for step in (4, 2, 1):
         x = x + roll(x, step)
     return x
+
+
+def both(pair):
+    return jnp.broadcast_to(pair[0:1] + pair[1:2], (SUB, 128))
 
 
 def wire(admittance, here, there):
@@ -136,7 +140,10 @@
 
     def message(self, source):
         near, far = self.condense(source)
-        return jnp.where(sublanes() < 4, near + roll(near, 4), far + roll(far, 4))
+        half = jnp.where(sublanes() < 4, near + roll(near, 4), far + roll(far, 4))
+        half = half + roll(half, -2)
+        half = half + roll(half, -1)
+        return half[0:1], half[4:5]
 
     def inside(self, source):
         sub = sublanes()
@@ -164,20 +171,14 @@
                 between = wire(self.admittance, part[4:5], parts[d + 1][3:4])
                 link = jnp.where(at == 2 * d + 1, between, link)
         factors = pcr_factor(ground, link)
-        upper = sublanes() < 4
         self.weights = []
         for kept in (2 * place, 2 * place + 1):
             row = pcr_apply(factors, jnp.where(at == kept, 1.0, 0.0))
-            self.weights.append(
-                [
-                    jnp.where(upper, row[2 * d : 2 * d + 1], row[2 * d + 1 : 2 * d + 2])
-                    for d in range(devices)
-                ]
-            )
+            self.weights.append([row[2 * d : 2 * d + 2] for d in range(devices)])
 
     def finish(self, messages, inside):
         first, last = (
-            total(functools.reduce(jnp.add, [w * m for w, m in zip(weights, messages)]))
+            both(functools.reduce(jnp.add, [w * m for w, m in zip(weights, messages)]))
             for weights in self.weights
         )
         return [
@@ -193,30 +194,35 @@
             pltpu.make_async_remote_copy(
                 src_ref=mine,
                 dst_ref=slots.at[place],
-                send_sem=send_sem.at[ahead - 1],
-                recv_sem=recv_sem.at[ahead - 1],
+                send_sem=send_sem,
+                recv_sem=recv_sem,
                 device_id={axis: lax.rem(place + ahead, devices)},
                 device_id_type=MESH,
             )
             for ahead in sorted(range(1, devices), key=lambda a: -min(a, devices - a))
         ]
         self.place, self.devices, self.mine, self.slots = place, devices, mine, slots
+        every = slots.at[pl.ds(0, devices - 1)]
+        self.received = pltpu.make_async_copy(every, every, recv_sem)
+        self.sent = pltpu.make_async_copy(every, every, send_sem)
 
     def start(self, value):
-        self.mine[...] = value
+        if isinstance(value, tuple):
+            for r, row in enumerate(value):
+                self.mine[r : r + 1, :] = row
+        else:
+            self.mine[...] = value
         for copy in self.copies:
             copy.start()
 
     def arrived(self):
-        for copy in self.copies:
-            copy.wait_recv()
+        self.received.wait()
         return [
             jnp.where(self.place == d, self.mine[...], self.slots[d]) for d in range(self.devices)
         ]
 
     def close(self):
-        for copy in self.copies:
-            copy.wait_send()
+        self.sent.wait()
 
 
 def kernel(
@@ -349,12 +355,19 @@
             line_x.weigh(share_x.arrived(), place_x)
             line_y = Line(ground_y, link_y, warmth_y, yward_admittance)
             share_y.start(line_y.coefficients)
+        else:
+            exchange_y[s - 1].close()
         inside = line_x.inside(source)
         half = line_x.finish(exchange_x[s].arrived(), inside)
         source = [2.0 * c * h - f + q for c, h, f, q in zip(store_x, half, source, load[s])]
         source_y = to_y(source)
         exchange_y[s].start(line_y.message(source_y))
+        exchange_x[s].close()
         if s == 0:
+            share_x.close()
+            share_y.close()
+            for sends, _, copy in halos:
+                pl.when(sends)(copy.wait_send)
             line_y.weigh(share_y.arrived(), place_y)
         inside = line_y.inside(source_y)
         drop = line_y.finish(exchange_y[s].arrived(), inside)
@@ -364,21 +377,18 @@
     for k, part in enumerate(to_x(drop)):
         out_ref[pl.ds(k, SUB, stride=depth_x), :] = part
 
-    for exchange in exchange_x + [share_x, share_y] + exchange_y:
-        exchange.close()
-    for sends, _, copy in halos:
-        pl.when(sends)(copy.wait_send)
+    exchange_y[-1].close()
 
 
 def local(count_x, count_y, sag, warmth, store, load, flags):
-    tile = (SUB, 128)
+    tile, pair = (SUB, 128), (2, 128)
     vmem = pl.BlockSpec(memory_space=pltpu.VMEM)
 
     def buffers(devices, shape):
         return [pltpu.VMEM(shape, jnp.float32), pltpu.VMEM((devices,) + shape, jnp.float32)]
 
-    def semaphores(devices):
-        return [pltpu.SemaphoreType.DMA((devices - 1,))] * 2
+    def semaphores():
+        return [pltpu.SemaphoreType.DMA] * 2
 
     return pl.pallas_call(
         functools.partial(kernel, count_x, count_y),
@@ -393,19 +403,14 @@
             pltpu.VMEM((2,) + tile, jnp.float32),
             pltpu.VMEM((2,) + tile, jnp.float32),
             *buffers(count_x, tile),
-            *buffers(count_x, tile),
-            *buffers(count_x, tile),
+            *buffers(count_x, pair),
+            *buffers(count_x, pair),
             *buffers(count_y, tile),
-            *buffers(count_y, tile),
-            *buffers(count_y, tile),
+            *buffers(count_y, pair),
+            *buffers(count_y, pair),
             pltpu.SemaphoreType.DMA((2,)),
             pltpu.SemaphoreType.DMA((2,)),
-            *semaphores(count_x),
-            *semaphores(count_x),
-            *semaphores(count_x),
-            *semaphores(count_y),
-            *semaphores(count_y),
-            *semaphores(count_y),
+            *(semaphores() * 6),
         ],
         compiler_params=pltpu.CompilerParams(
             collective_id=0, has_side_effects=True, vmem_limit_bytes=16 * 2**20

time: 22.3 us -> 21.5 us (0.964)
  Pallas kernels: 21.5 us -> 20.7 us
    pallas_call x1, Pallas kernels: 21.5 us -> 20.7 us  [local(): pl.pallas_call(functools.partial(kernel, count_x, count_y), out_shape=plt...]
where the time goes in v3:
time: 21.5 us; the launch traced here: 21.3 us
  Pallas kernels  20.7 us (96%)
  local copies, waits for them, and re-layouts  0.63 us (3%)
    pallas_call x1, Pallas kernels, local(): pl.pallas_call(functools.partial(kernel, count_x, count_y), out_shape=plt...  20.7 us
    unnamed x1, local copies, waits for them, and re-layouts  0.63 us

profile of v3, /device:TPU:0, one launch (start us, length us, event | category | flops | bytes accessed | tf_op | source)
XLA Modules:
  0.0 21.3 jit_solution(1478457585588518831)
XLA Ops:
  0.0 20.7 %shard_map.55 = f32[128,128]{1,0:T(8,128)S(1)} custom-call(f32[128,128]{1,0:T(8,128)} %sag_hbm.1, f32[128,128]{1,0:T(8,128)} %warmth_hbm.1, f32[128,128]{1,0:T(8,128)} %store_hbm.1, f32[2,128,128]{2,1,0:T(8,128)} %load_hbm.1, s32[4,4]{1,0:T(4,128)} %flag_hbm.1), custom_call_target="tpu_custom_call" | custom-call | tf_op jit(solution)/shard_map/pallas_call | solution.py:393
  20.7 0.6 %copy.7 = f32[128,128]{1,0:T(8,128)} copy(f32[128,128]{1,0:T(8,128)S(1)} %shard_map.55) | data formatting | bytes 131072

commit v4 on v3

--- a/solution.py
+++ b/solution.py
@@ -33,6 +33,12 @@
     for step in (4, 2, 1):
         x = x + roll(x, step)
     return x
+
+
+def tree(parts):
+    while len(parts) > 1:
+        parts = [functools.reduce(jnp.add, parts[k : k + 2]) for k in range(0, len(parts), 2)]
+    return parts[0]
 
 
 def both(pair):
@@ -176,15 +182,29 @@
             row = pcr_apply(factors, jnp.where(at == kept, 1.0, 0.0))
             self.weights.append([row[2 * d : 2 * d + 2] for d in range(devices)])
 
-    def finish(self, messages, inside):
-        first, last = (
-            both(functools.reduce(jnp.add, [w * m for w, m in zip(weights, messages)]))
-            for weights in self.weights
-        )
+    def ends(self, messages):
         return [
-            u + near * first + far * last
-            for u, near, far in zip(inside, self.near, self.far)
+            both(tree([w * m for w, m in zip(weights, messages)])) for weights in self.weights
         ]
+
+    def response(self, scale):
+        return [c * p for c, p in zip(scale, self.near)], [c * p for c, p in zip(scale, self.far)]
+
+
+def respond(base, response, ends):
+    first, last = ends
+    return [u + (p * first + q * last) for u, p, q in zip(base, *response)]
+
+
+def partner(place, turn, devices):
+    if devices & (devices - 1):
+        return lax.rem(place + turn + 1, devices)
+    flips, bit, other = devices - 1 - turn, 1, 0
+    while bit < devices:
+        here = lax.rem(lax.div(place, bit), 2)
+        other = other + bit * (1 - here if flips & bit else here)
+        bit *= 2
+    return other
 
 
 class Exchange:
@@ -196,10 +216,10 @@
                 dst_ref=slots.at[place],
                 send_sem=send_sem,
                 recv_sem=recv_sem,
-                device_id={axis: lax.rem(place + ahead, devices)},
+                device_id={axis: partner(place, turn, devices)},
                 device_id_type=MESH,
             )
-            for ahead in sorted(range(1, devices), key=lambda a: -min(a, devices - a))
+            for turn in range(devices - 1)
         ]
         self.place, self.devices, self.mine, self.slots = place, devices, mine, slots
         every = slots.at[pl.ds(0, devices - 1)]
@@ -244,6 +264,15 @@
     sub = sublanes()
     lane = lax.broadcasted_iota(jnp.int32, (SUB, 128), 1)
 
+    halo_y[...] = jnp.zeros_like(halo_y)
+    barrier = pltpu.get_barrier_semaphore()
+    for axis, place, devices in (("gy", place_y, count_y), ("gx", place_x, count_x)):
+        for turn in range(devices - 1):
+            pl.semaphore_signal(
+                barrier, inc=1,
+                device_id={axis: partner(place, turn, devices)}, device_id_type=MESH,
+            )
+
     fetches = [
         pltpu.make_async_copy(src, dst, fetch_sem.at[k])
         for k, (src, dst) in enumerate([
@@ -253,14 +282,6 @@
     ]
     for fetch in fetches:
         fetch.start()
-    halo_y[...] = jnp.zeros_like(halo_y)
-    barrier = pltpu.get_barrier_semaphore()
-    for axis, place, devices in (("gx", place_x, count_x), ("gy", place_y, count_y)):
-        for ahead in range(1, devices):
-            pl.semaphore_signal(
-                barrier, inc=1,
-                device_id={axis: lax.rem(place + ahead, devices)}, device_id_type=MESH,
-            )
 
     def split(ref, depth):
         return [ref[pl.ds(k, SUB, stride=depth), :] for k in range(depth)]
@@ -320,46 +341,55 @@
     share_x = Exchange("gx", count_x, mine_xc, slots_xc, xc_send, xc_recv)
     share_x.start(line_x.coefficients)
 
+    next_y = warmth_y[1:] + [roll(warmth_y[0], -1)]
+    link_y = [wire(yward_admittance, a, b) for a, b in zip(warmth_y, next_y)]
+    line_y = Line(ground_y, link_y, warmth_y, yward_admittance)
+    share_y = Exchange("gy", count_y, mine_yc, slots_yc, yc_send, yc_recv)
+    share_y.start(line_y.coefficients)
+    fetches[4].wait()
+    load = [split(load_ref.at[s], depth_x) for s in range(STEPS)]
+    twice_x = [2.0 * c for c in store_x]
+    twice_y = [2.0 * c for c in store_y]
+    flow = [g * (a - b) for g, a, b in zip(link_y[:-1], sag_y[:-1], sag_y[1:])]
+    kept = [c * v for c, v in zip(store_y, sag_y)]
+    kept[0] = kept[0] - cushion_y * sag_y[0]
+    inner = [k - (o - i) for k, o, i in zip(kept[1:-1], flow[1:], flow[:-1])]
+
     for _, receives, copy in halos:
         pl.when(receives)(copy.wait_recv)
 
     last_y = (sub == SUB - 1) & (place_y == count_y - 1)
     first_y = (sub == 0) & (place_y == 0)
-    next_y = warmth_y[1:] + [after(warmth_y[0], halo_y[0, 0:1])]
-    link_y = [wire(yward_admittance, a, b) for a, b in zip(warmth_y, next_y)]
-    link_y[-1] = jnp.where(last_y, 0.0, link_y[-1])
-    next_sag = sag_y[1:] + [after(sag_y[0], halo_y[0, 1:2])]
-    flow = [g * (a - b) for g, a, b in zip(link_y, sag_y, next_sag)]
+    next_warmth = after(warmth_y[0], halo_y[0, 0:1])
+    next_sag = after(sag_y[0], halo_y[0, 1:2])
+    outflow = wire(yward_admittance, warmth_y[-1], next_warmth) * (sag_y[-1] - next_sag)
+    outflow = jnp.where(last_y, 0.0, outflow)
     inflow = wire(yward_admittance, halo_y[1, 0:1], warmth_y[0]) * (halo_y[1, 1:2] - sag_y[0])
     inflow = jnp.where(first_y, 0.0, inflow)
-    flow_in = [jnp.where(sub == 0, inflow, roll(flow[-1], 1))] + flow[:-1]
-    source_y = [c * v - (o - i) for c, v, o, i in zip(store_y, sag_y, flow, flow_in)]
-    source_y[0] = source_y[0] - cushion_y * sag_y[0]
+    inflow = jnp.where(sub == 0, inflow, roll(outflow, 1))
+    source_y = [kept[0] - (flow[0] - inflow), *inner, kept[-1] - (outflow - flow[-1])]
 
     exchange_x = [
         Exchange("gx", count_x, mine_x0, slots_x0, x0_send, x0_recv),
         Exchange("gx", count_x, mine_x1, slots_x1, x1_send, x1_recv),
     ]
-    share_y = Exchange("gy", count_y, mine_yc, slots_yc, yc_send, yc_recv)
     exchange_y = [
         Exchange("gy", count_y, mine_y0, slots_y0, y0_send, y0_recv),
         Exchange("gy", count_y, mine_y1, slots_y1, y1_send, y1_recv),
     ]
 
-    fetches[4].wait()
-    load = [split(load_ref.at[s], depth_x) for s in range(STEPS)]
     source = [a + b for a, b in zip(to_x(source_y), load[0])]
     for s in range(STEPS):
         exchange_x[s].start(line_x.message(source))
         if s == 0:
             line_x.weigh(share_x.arrived(), place_x)
-            line_y = Line(ground_y, link_y, warmth_y, yward_admittance)
-            share_y.start(line_y.coefficients)
         else:
             exchange_y[s - 1].close()
         inside = line_x.inside(source)
-        half = line_x.finish(exchange_x[s].arrived(), inside)
-        source = [2.0 * c * h - f + q for c, h, f, q in zip(store_x, half, source, load[s])]
+        base = [d * u - f + q for d, u, f, q in zip(twice_x, inside, source, load[s])]
+        if s == 0:
+            response_x = line_x.response(twice_x)
+        source = respond(base, response_x, line_x.ends(exchange_x[s].arrived()))
         source_y = to_y(source)
         exchange_y[s].start(line_y.message(source_y))
         exchange_x[s].close()
@@ -370,10 +400,13 @@
                 pl.when(sends)(copy.wait_send)
             line_y.weigh(share_y.arrived(), place_y)
         inside = line_y.inside(source_y)
-        drop = line_y.finish(exchange_y[s].arrived(), inside)
         if s + 1 < STEPS:
-            carried = [2.0 * c * v - f for c, v, f in zip(store_y, drop, source_y)]
+            base = [d * u - f for d, u, f in zip(twice_y, inside, source_y)]
+            if s == 0:
+                response_y = line_y.response(twice_y)
+            carried = respond(base, response_y, line_y.ends(exchange_y[s].arrived()))
             source = [a + b for a, b in zip(to_x(carried), load[s + 1])]
+    drop = respond(inside, (line_y.near, line_y.far), line_y.ends(exchange_y[-1].arrived()))
     for k, part in enumerate(to_x(drop)):
         out_ref[pl.ds(k, SUB, stride=depth_x), :] = part
 

time: 21.5 us -> 21.4 us (level)
  no operation moved by 1% of the time
where the time goes in v4:
time: 21.4 us; the launch traced here: 21.2 us
  Pallas kernels  20.6 us (96%)
  local copies, waits for them, and re-layouts  0.63 us (3%)
    pallas_call x1, Pallas kernels, local(): pl.pallas_call(functools.partial(kernel, count_x, count_y), out_shape=plt...  20.6 us
    unnamed x1, local copies, waits for them, and re-layouts  0.63 us

profile of v4, /device:TPU:0, one launch (start us, length us, event | category | flops | bytes accessed | tf_op | source)
XLA Modules:
  0.0 21.2 jit_solution(12019706422842090967)
XLA Ops:
  0.0 20.6 %shard_map.55 = f32[128,128]{1,0:T(8,128)S(1)} custom-call(f32[128,128]{1,0:T(8,128)} %sag_hbm.1, f32[128,128]{1,0:T(8,128)} %warmth_hbm.1, f32[128,128]{1,0:T(8,128)} %store_hbm.1, f32[2,128,128]{2,1,0:T(8,128)} %load_hbm.1, s32[4,4]{1,0:T(4,128)} %flag_hbm.1), custom_call_target="tpu_custom_call" | custom-call | tf_op jit(solution)/shard_map/pallas_call | solution.py:426
  20.6 0.6 %copy.7 = f32[128,128]{1,0:T(8,128)} copy(f32[128,128]{1,0:T(8,128)S(1)} %shard_map.55) | data formatting | bytes 131072

commit v5 on v4

--- a/solution.py
+++ b/solution.py
@@ -196,6 +196,17 @@
     return [u + (p * first + q * last) for u, p, q in zip(base, *response)]
 
 
+def carry(base, ends, ref):
+    both_ends = jnp.concatenate(ends, 1)
+    return tuple(
+        row + jnp.dot(
+            both_ends, ref[k],
+            precision=lax.Precision.HIGHEST, preferred_element_type=jnp.float32,
+        )[0:1]
+        for k, row in enumerate(base)
+    )
+
+
 def partner(place, turn, devices):
     if devices & (devices - 1):
         return lax.rem(place + turn + 1, devices)
@@ -250,7 +261,7 @@
     sag_hbm, warmth_hbm, store_hbm, load_hbm, flag_hbm,
     out_ref,
     sag_ref, warmth_ref, store_ref, load_ref, flag_ref, fetch_sem,
-    turn_ref, halo_y, edge_y,
+    turn_ref, to_y_ref, to_x_ref, halo_y, edge_y,
     mine_xc, slots_xc, mine_x0, slots_x0, mine_x1, slots_x1,
     mine_yc, slots_yc, mine_y0, slots_y0, mine_y1, slots_y1,
     halo_send, halo_recv,
@@ -379,19 +390,24 @@
     ]
 
     source = [a + b for a, b in zip(to_x(source_y), load[0])]
+    exchange_x[0].start(line_x.message(source))
+    line_x.weigh(share_x.arrived(), place_x)
     for s in range(STEPS):
-        exchange_x[s].start(line_x.message(source))
-        if s == 0:
-            line_x.weigh(share_x.arrived(), place_x)
-        else:
+        if s > 0:
             exchange_y[s - 1].close()
         inside = line_x.inside(source)
         base = [d * u - f + q for d, u, f, q in zip(twice_x, inside, source, load[s])]
         if s == 0:
             response_x = line_x.response(twice_x)
-        source = respond(base, response_x, line_x.ends(exchange_x[s].arrived()))
-        source_y = to_y(source)
-        exchange_y[s].start(line_y.message(source_y))
+            for half, response in enumerate(response_x):
+                for k, part in enumerate(to_y(response)):
+                    at = pl.ds(128 * half + k, SUB, stride=depth_y)
+                    to_y_ref[0, at, :] = line_y.near[k] * part
+                    to_y_ref[1, at, :] = line_y.far[k] * part
+        message = line_y.message(to_y(base))
+        ends = line_x.ends(exchange_x[s].arrived())
+        exchange_y[s].start(carry(message, ends, to_y_ref))
+        source_y = to_y(respond(base, response_x, ends))
         exchange_x[s].close()
         if s == 0:
             share_x.close()
@@ -404,7 +420,15 @@
             base = [d * u - f for d, u, f in zip(twice_y, inside, source_y)]
             if s == 0:
                 response_y = line_y.response(twice_y)
-            carried = respond(base, response_y, line_y.ends(exchange_y[s].arrived()))
+                for half, response in enumerate(response_y):
+                    for k, part in enumerate(to_x(response)):
+                        at = pl.ds(128 * half + SUB * k, SUB)
+                        to_x_ref[0, at, :] = line_x.near[k] * part
+                        to_x_ref[1, at, :] = line_x.far[k] * part
+            message = line_x.message([a + b for a, b in zip(to_x(base), load[s + 1])])
+            ends = line_y.ends(exchange_y[s].arrived())
+            exchange_x[s + 1].start(carry(message, ends, to_x_ref))
+            carried = respond(base, response_y, ends)
             source = [a + b for a, b in zip(to_x(carried), load[s + 1])]
     drop = respond(inside, (line_y.near, line_y.far), line_y.ends(exchange_y[-1].arrived()))
     for k, part in enumerate(to_x(drop)):
@@ -433,6 +457,8 @@
             pltpu.SMEM(flags.shape, jnp.int32),
             pltpu.SemaphoreType.DMA((5,)),
             pltpu.VMEM((sag.shape[1], sag.shape[0]), jnp.float32),
+            pltpu.VMEM((2, 256, 128), jnp.float32),
+            pltpu.VMEM((2, 256, 128), jnp.float32),
             pltpu.VMEM((2,) + tile, jnp.float32),
             pltpu.VMEM((2,) + tile, jnp.float32),
             *buffers(count_x, tile),

time: 21.4 us -> 21.7 us (1.014)
  Pallas kernels: 20.6 us -> 20.9 us
    pallas_call x1, Pallas kernels: 20.6 us -> 20.9 us  [local(): pl.pallas_call(functools.partial(kernel, count_x, count_y), out_shape=plt...]
where the time goes in v5:
time: 21.7 us; the launch traced here: 21.5 us
  Pallas kernels  20.9 us (96%)
  local copies, waits for them, and re-layouts  0.63 us (3%)
    pallas_call x1, Pallas kernels, local(): pl.pallas_call(functools.partial(kernel, count_x, count_y), out_shape=plt...  20.9 us
    unnamed x1, local copies, waits for them, and re-layouts  0.63 us

profile of v5, /device:TPU:0, one launch (start us, length us, event | category | flops | bytes accessed | tf_op | source)
XLA Modules:
  0.0 21.5 jit_solution(16873328727575605786)
XLA Ops:
  0.0 20.9 %shard_map.55 = f32[128,128]{1,0:T(8,128)S(1)} custom-call(f32[128,128]{1,0:T(8,128)} %sag_hbm.1, f32[128,128]{1,0:T(8,128)} %warmth_hbm.1, f32[128,128]{1,0:T(8,128)} %store_hbm.1, f32[2,128,128]{2,1,0:T(8,128)} %load_hbm.1, s32[4,4]{1,0:T(4,128)} %flag_hbm.1), custom_call_target="tpu_custom_call" | custom-call | tf_op jit(solution)/shard_map/pallas_call | solution.py:450
  20.9 0.6 %copy.7 = f32[128,128]{1,0:T(8,128)} copy(f32[128,128]{1,0:T(8,128)S(1)} %shard_map.55) | data formatting | bytes 131072

commit v6 on v4

--- a/solution.py
+++ b/solution.py
@@ -345,7 +345,6 @@
     link_y = [wire(yward_admittance, a, b) for a, b in zip(warmth_y, next_y)]
     line_y = Line(ground_y, link_y, warmth_y, yward_admittance)
     share_y = Exchange("gy", count_y, mine_yc, slots_yc, yc_send, yc_recv)
-    share_y.start(line_y.coefficients)
     fetches[4].wait()
     load = [split(load_ref.at[s], depth_x) for s in range(STEPS)]
     twice_x = [2.0 * c for c in store_x]
@@ -382,6 +381,7 @@
     for s in range(STEPS):
         exchange_x[s].start(line_x.message(source))
         if s == 0:
+            share_y.start(line_y.coefficients)
             line_x.weigh(share_x.arrived(), place_x)
         else:
             exchange_y[s - 1].close()
@@ -406,11 +406,10 @@
                 response_y = line_y.response(twice_y)
             carried = respond(base, response_y, line_y.ends(exchange_y[s].arrived()))
             source = [a + b for a, b in zip(to_x(carried), load[s + 1])]
+    exchange_y[-1].close()
     drop = respond(inside, (line_y.near, line_y.far), line_y.ends(exchange_y[-1].arrived()))
     for k, part in enumerate(to_x(drop)):
         out_ref[pl.ds(k, SUB, stride=depth_x), :] = part
-
-    exchange_y[-1].close()
 
 
 def local(count_x, count_y, sag, warmth, store, load, flags):

time: 21.4 us -> 21.4 us (level)
  no operation moved by 1% of the time
where the time goes in v6:
time: 21.4 us; the launch traced here: 21.2 us
  Pallas kernels  20.6 us (96%)
  local copies, waits for them, and re-layouts  0.63 us (3%)
    pallas_call x1, Pallas kernels, local(): pl.pallas_call(functools.partial(kernel, count_x, count_y), out_shape=plt...  20.6 us
    unnamed x1, local copies, waits for them, and re-layouts  0.63 us

profile of v6, /device:TPU:0, one launch (start us, length us, event | category | flops | bytes accessed | tf_op | source)
XLA Modules:
  0.0 21.2 jit_solution(11316107460506475682)
XLA Ops:
  0.0 20.6 %shard_map.55 = f32[128,128]{1,0:T(8,128)S(1)} custom-call(f32[128,128]{1,0:T(8,128)} %sag_hbm.1, f32[128,128]{1,0:T(8,128)} %warmth_hbm.1, f32[128,128]{1,0:T(8,128)} %store_hbm.1, f32[2,128,128]{2,1,0:T(8,128)} %load_hbm.1, s32[4,4]{1,0:T(4,128)} %flag_hbm.1), custom_call_target="tpu_custom_call" | custom-call | tf_op jit(solution)/shard_map/pallas_call | solution.py:425
  20.6 0.6 %copy.7 = f32[128,128]{1,0:T(8,128)} copy(f32[128,128]{1,0:T(8,128)S(1)} %shard_map.55) | data formatting | bytes 131072
